TPU v7x, 32 devices: a whole 2x2x4 slice. The times are simulated.
32 devices in a mesh: context: 4 (over z), head: 8 (over y, x, core).
Axes of the slice: x: 2, y: 2, z: 4, core: 2. Of those that a mesh axis runs over, the one named last changes fastest.
Arguments:
- x_in: bfloat16 [4096, 2048], P('context', 'head'), may hold values from -6 to 6
- bc_in: bfloat16 [4096, 4096], P('context'), may hold values from -6 to 6
- z_in: bfloat16 [4096, 2048], P('context', 'head'), may hold values from -6 to 6
- dt_in: bfloat16 [32, 4096], P('head', 'context'), may hold values from -4 to 4
- conv_x_w: float32 [4, 2048], P(None, 'head'), may hold values from -3 to 3
- conv_x_b: float32 [2048], P('head'), may hold values from -1.5 to 1.5
- conv_bc_w: float32 [4, 4096], replicated, may hold values from -3 to 3
- conv_bc_b: float32 [4096], replicated, may hold values from -1.5 to 1.5
- dt_bias: float32 [32], P('head'), may hold values from -3.5 to -2.5
- a_log: float32 [32], P('head'), may hold values from -12 to 0
- skip_gain: float32 [32], P('head'), may hold values from 1 to 4
- norm_w: float32 [2048], P('head'), may hold values from 0.5 to 1.5
- doc_len: int32 [16], replicated, may hold values from 1 to 2048, 4096 in all
Outputs:
- ssd_out: bfloat16 [4096, 2048], P('context', 'head')
Inputs may be any that keep to these rules, and one draw needn't show every extreme that they name: `doc_len`: the lengths sum to 4096; the longest is exactly 2048.
All inputs are finite; a program needn't handle non-finite values.
Results may differ from a plain program's by a relative error of at most 0.0034.
Values may be sent and summed in bfloat16 or wider, within the bound.
A program may use at most 64 MiB of HBM per device.

v0:
```python
import jax
import jax.numpy as jnp
from jax import lax
from jax.sharding import PartitionSpec as P

HEAD_DIM = 64
STATE = 256
GROUPS = 8
CONV = 4
BLOCK = 256


exact_mode = lax.Precision.HIGHEST
norm_floor = 1e-05


def from_behind(shard, axis, by):
    count = lax.axis_size(axis)
    pairs = [(i, i + by) for i in range(count) if 0 <= i + by < count]
    return lax.ppermute(shard, axis, pairs)


def doc_marks(doc_len, positions):
    doc_ends = jnp.cumsum(doc_len)
    begins = doc_ends - doc_len
    segment = jnp.sum((doc_ends[None, :] <= positions[:, None]).astype(jnp.int32), axis=1)
    opening = jnp.sum((begins[None, :] == positions[:, None]).astype(jnp.int32), axis=1)
    return (segment, opening)


def conv_silu(extended, segment_ext, weights, biases, rows_count):
    newest = segment_ext[CONV - 1 : CONV - 1 + rows_count]
    summed = jnp.zeros((rows_count, extended.shape[1]), jnp.float32) + biases[None, :]
    for offset in range(CONV):
        same_doc = (segment_ext[offset : offset + rows_count] == newest).astype(jnp.float32)
        summed = (
            summed
            + weights[offset][None, :]
            * extended[offset : offset + rows_count].astype(jnp.float32)
            * same_doc[:, None]
        )
    return jax.nn.silu(summed).astype(jnp.bfloat16)


def shards(
    x_in,
    bc_in,
    z_in,
    dt_in,
    conv_x_w,
    conv_x_b,
    conv_bc_w,
    conv_bc_b,
    dt_bias,
    a_log,
    skip_gain,
    norm_w,
    doc_len,
):
    rows_here = x_in.shape[0]
    heads_here = dt_in.shape[0]
    width_here = x_in.shape[1]
    heads_total = heads_here * lax.axis_size("head")
    per_group = heads_total // GROUPS
    group_index = lax.axis_index("head") * heads_here // per_group
    b_raw = lax.dynamic_slice_in_dim(bc_in, group_index * STATE, STATE, 1)
    c_raw = lax.dynamic_slice_in_dim(bc_in, (GROUPS + group_index) * STATE, STATE, 1)
    raw_rows = jnp.concatenate([x_in, b_raw, c_raw], axis=1)
    weights = jnp.concatenate(
        [
            conv_x_w,
            lax.dynamic_slice_in_dim(conv_bc_w, group_index * STATE, STATE, 1),
            lax.dynamic_slice_in_dim(conv_bc_w, (GROUPS + group_index) * STATE, STATE, 1),
        ],
        axis=1,
    )
    biases = jnp.concatenate(
        [
            conv_x_b,
            lax.dynamic_slice_in_dim(conv_bc_b, group_index * STATE, STATE, 0),
            lax.dynamic_slice_in_dim(conv_bc_b, (GROUPS + group_index) * STATE, STATE, 0),
        ],
        axis=0,
    )
    before = from_behind(raw_rows[rows_here - (CONV - 1) :], "context", 1)
    extended = jnp.concatenate([before, raw_rows], axis=0)
    first_pos = lax.axis_index("context") * rows_here
    positions_ext = first_pos - (CONV - 1) + jnp.arange(rows_here + CONV - 1, dtype=jnp.int32)
    segment_ext, opening_ext = doc_marks(doc_len, positions_ext)
    mixed = conv_silu(extended, segment_ext, weights, biases, rows_here)
    segment = segment_ext[CONV - 1 :]
    opening = opening_ext[CONV - 1 :]
    blocks = rows_here // BLOCK
    x_vals = mixed[:, :width_here].astype(jnp.float32).reshape(blocks, BLOCK, heads_here, HEAD_DIM)
    b_vals = (
        mixed[:, width_here : width_here + STATE].astype(jnp.float32).reshape(blocks, BLOCK, STATE)
    )
    c_vals = mixed[:, width_here + STATE :].astype(jnp.float32).reshape(blocks, BLOCK, STATE)
    step_size = jax.nn.softplus(dt_in.astype(jnp.float32) + dt_bias[:, None])
    log_decay = (step_size * (-jnp.exp(a_log))[:, None]).reshape(heads_here, blocks, BLOCK)
    running = jnp.cumsum(log_decay, axis=2)
    step_blocks = jnp.transpose(step_size.reshape(heads_here, blocks, BLOCK), (1, 2, 0))
    weighted = x_vals * step_blocks[..., None]
    seg_blocks = segment.reshape(blocks, BLOCK)
    alive_mask = jnp.cumsum(opening.reshape(blocks, BLOCK), axis=1) == 0
    lower_tri = jnp.arange(BLOCK)[:, None] >= jnp.arange(BLOCK)[None, :]
    same_block = (seg_blocks[:, :, None] == seg_blocks[:, None, :]) & lower_tri[None]
    inner_prod = jnp.einsum("ctn,csn->cts", c_vals, b_vals, precision=exact_mode)
    gap_logs = jnp.minimum(running[:, :, :, None] - running[:, :, None, :], 0.0)
    mixing = jnp.where(same_block[None], jnp.exp(gap_logs), 0.0) * inner_prod[None]
    intra_out = jnp.einsum("hcts,cshp->cthp", mixing, weighted, precision=exact_mode)
    tail_weight = jnp.where(
        (seg_blocks == seg_blocks[:, -1:])[None], jnp.exp(running[:, :, -1:] - running), 0.0
    )
    tail_blocks = jnp.transpose(tail_weight, (1, 2, 0))
    summaries = jnp.einsum(
        "cshp,csn->chpn", weighted * tail_blocks[..., None], b_vals, precision=exact_mode
    )
    carry_decay = jnp.transpose(
        jnp.exp(running[:, :, -1]) * alive_mask[None, :, -1].astype(jnp.float32)
    )

    def advance(carry_now, inputs):
        state_now, decay_now = carry_now
        summary, factor = inputs
        return (
            (factor[:, None, None] * state_now + summary, decay_now * factor),
            (state_now, decay_now),
        )

    zero_state = jnp.zeros((heads_here, HEAD_DIM, STATE), jnp.float32)
    unit_decay = jnp.ones((heads_here,), jnp.float32)
    (local_end, local_decay), (local_in, decay_in) = lax.scan(
        advance, (zero_state, unit_decay), (summaries, carry_decay)
    )

    def pass_on(step_index, entering):
        return from_behind(local_decay[:, None, None] * entering + local_end, "context", 1)

    entering = lax.fori_loop(0, lax.axis_size("context") - 1, pass_on, zero_state)
    incoming = local_in + decay_in[:, :, None, None] * entering[None]
    entry_scale = jnp.transpose(alive_mask[None].astype(jnp.float32) * jnp.exp(running), (1, 2, 0))
    from_state = (
        jnp.einsum("ctn,chpn->cthp", c_vals, incoming, precision=exact_mode)
        * entry_scale[..., None]
    )
    outputs = intra_out + from_state + skip_gain[None, None, :, None] * x_vals
    outputs = outputs.reshape(rows_here, width_here)
    gated_out = outputs * jax.nn.silu(z_in.astype(jnp.float32))
    squares = jnp.sum(gated_out * gated_out, axis=1)
    total_squares = lax.psum(squares, "head")
    mean_square = total_squares / (heads_total * HEAD_DIM)
    result = gated_out * lax.rsqrt(mean_square + norm_floor)[:, None] * norm_w[None, :]
    return result.astype(jnp.bfloat16)


def solution(mesh):
    return jax.shard_map(
        shards,
        mesh=mesh,
        in_specs=(
            P("context", "head"),
            P("context", None),
            P("context", "head"),
            P("head", "context"),
            P(None, "head"),
            P("head"),
            P(),
            P(),
            P("head"),
            P("head"),
            P("head"),
            P("head"),
            P(),
        ),
        out_specs=P("context", "head"),
        check_vma=False,
    )
```

profile of v0, /device:TPU:0, one launch (start us, length us, event | category | flops | bytes accessed | tf_op | source)
XLA Modules:
  0.0 79.3 jit_solution(18223557881293850799)
XLA Ops:
  0.1 1.3 %constant_dynamic-slice_fusion.2 = (bf16[1024,256]{1,0:T(8,128)(2,1)S(1)}, bf16[1024,256]{1,0:T(8,128)(2,1)S(1)}) fusion(bf16[1024,4096]{1,0:T(8,128)(2,1)} %param.18, s32[]{:T(128)S(6)} %select_n.28, s32[]{:T(128)S(6)} %select_n.29), kind=kLoop, calls=%fused_computation.77 | loop fusion | bytes 2097160 | tf_op jit(solution)/shard_map/dynamic_slice | solution.py:66
  1.4 1.2 %pad_maximum_fusion = bf16[1024,768]{1,0:T(8,128)(2,1)S(1)} fusion(bf16[1024,256]{1,0:T(8,128)(2,1)S(1)} %get-tuple-element.162, bf16[1024,256]{1,0:T(8,128)(2,1)S(1)} %get-tuple-element.161, bf16[1024,256]{1,0:T(8,128)(2,1)} %param.17), kind=kLoop, calls=%fused_computation.21 | loop fusion | flops 4718592 | bytes 3145728 | tf_op jit(solution)/shard_map/concatenate | solution.py:68
  2.6 4.9 %collective-permute-start.1 = (bf16[3,768]{1,0:T(4,128)(2,1)S(1)}, bf16[3,768]{1,0:T(4,128)(2,1)S(1)}, u32[]{:S(2)}, u32[]{:S(2)}) collective-permute-start(bf16[3,768]{1,0:T(4,128)(2,1)S(1)} %slice.96), channel_id=1, source_target_pairs={{0,8},{8,16},{16,24},{1,9},{9,17},{17,25},{2,10},{10,18},{18,26},{... | collective-permute-start | bytes 13832 | tf_op jit(solution)/shard_map/ppermute | solution.py:20
  7.6 0.1 copy.65
  7.7 0.1 reduce.1
  7.9 0.1 convert_reduce_fusion
  8.0 0.1 fusion.32
  8.2 0.7 constant_dynamic-slice_fusion.4
  8.9 0.8 fusion.38
  9.8 1.2 %reduce-window.31 = s32[4,2,128]{2,1,0:T(2,128)S(1)} reduce-window(s32[4,2,128]{2,1,0:T(2,128)S(1)} %bitcast.65, s32[]{:T(128)} %copy.122), window={size=1x1x128 pad=0_0x0_0x127_0}, to_apply=%region_5.6 | reduce-window | flops 130048 | bytes 8196 | tf_op jit(solution)/shard_map/reduce-window.3
  11.0 0.1 slice.114
  11.1 0.1 copy.73
  11.2 0.1 copy.74
  11.3 0.1 compare_bitcast_fusion
  11.4 0.1 broadcast_multiply_fusion.2
  11.6 4.8 %reduce-window.24 = f32[4,4,2,128]{3,2,1,0:T(2,128)S(1)} reduce-window(f32[4,4,2,128]{3,2,1,0:T(2,128)S(1)} %reshape.175, f32[]{:T(128)} %constant.82.clone.1), window={size=1x1x1x128 pad=0_0x0_0x0_0x127_0}, to_apply=%region_2.3 | reduce-window | flops 520192 | bytes 32772 | tf_op jit(solution)/shard_map/reduce-window.1
  16.4 0.1 slice.108
  16.5 0.1 copy.67
  16.6 0.1 copy.68
  16.7 0.1 broadcast_add_fusion
  17.0 0.2 slice_reduce_fusion.4
  17.2 1.0 %compare_and_fusion = pred[4,256,256]{2,1,0:T(8,128)(4,1)} fusion(s32[4,256]{1,0:T(4,128)S(1)} %eq.70, pred[256,256]{1,0:T(8,128)(4,1)S(1)} %iota_compare_fusion), kind=kLoop, calls=%fused_computation.40 | loop fusion | flops 524288 | bytes 331776 | tf_op jit(solution)/shard_map/and | solution.py:107
  18.1 0.1 copy.84
  18.2 0.1 broadcast_compare_fusion
  18.3 0.2 convert_reduce_fusion.2
  18.5 0.1 select_bitcast_fusion
  18.7 0.1 copy.76
  18.8 1.0 %copy.80 = bf16[1024,256]{0,1:T(8,128)(2,1)} copy(bf16[1024,256]{1,0:T(8,128)(2,1)S(1)} %copy-done.2) | data formatting | bytes 1048576 | tf_op args[2]
  19.8 0.4 maximum_maximum_fusion
  20.2 3.0 %multiply_convert_fusion = bf16[1024,768]{1,0:T(8,128)(2,1)S(1)} fusion(bf16[1027,768]{1,0:T(8,128)(2,1)S(1)} %maximum_maximum_fusion, f32[768]{0:T(1024)S(1)} %get-tuple-element.125, f32[1024]{0:T(1024)S(1)} %get-tuple-element.173, f32[768]{0:T(1024)S(1)} %get-tuple-element.126, f32[1024]{0:T(1024)S(1)} %get-tuple-element.174, ...), kind=kLoop, calls=%fused_computation.14 | loop fusion | flops 19660800 | bytes 7891968 | tf_op jit(solution)/shard_map/convert_element_type | solution.py:42
  23.1 0.1 slice_convert_fusion
  23.3 0.3 copy.66
  23.6 0.5 reshape.183
  24.1 1.3 %broadcast_multiply_fusion = (f32[4,256,4,64]{1,0,3,2:T(4,128)S(1)}, f32[4,256,4,64]{1,0,3,2:T(4,128)}) fusion(f32[4,256,4]{1,0,2:T(4,128)S(1)} %select_bitcast_fusion, f32[4,256,4,64]{1,0,3,2:T(4,128)S(1)} %reshape.183, f32[4,256,4]{1,0,2:T(4,128)S(1)} %bitcast.63), kind=kLoop, calls=%fused_computation.44 | loop fusion | flops 524288 | bytes 3178496 | tf_op jit(solution)/shard_map/mul | solution.py:117
  25.4 0.7 fusion.23
  26.1 3.6 %while.28 = (s32[]{:T(128)}, f32[4,64,256]{2,1,0:T(8,128)S(1)}, f32[4]{0:T(128)S(1)}, f32[4,4,64,256]{3,2,1,0:T(8,128)}, f32[4,4]{1,0:T(4,128)S(1)}, /*index=5*/...) while((s32[]{:T(128)}, f32[4,64,256]{2,1,0:T(8,128)S(1)}, ...), condition=%wide.region_8.9_spmd.clone, body=%wide.region_7.8_spmd.clone.sunk | while | flops 262155 | bytes 1310977 | solution.py:133
  26.1 0.7 bitcast_dynamic-update-slice_fusion.2
  26.9 0.1 bitcast_add_fusion.2
  27.0 0.7 bitcast_dynamic-update-slice_fusion.2
  27.8 0.1 bitcast_add_fusion.2
  27.9 0.7 bitcast_dynamic-update-slice_fusion.2
  28.7 0.1 bitcast_add_fusion.2
  28.8 0.7 bitcast_dynamic-update-slice_fusion.2
  29.6 0.1 bitcast_add_fusion.2
  29.7 0.3 fusion.39
  30.0 6.4 %fusion.16 = f32[4,256,4,64]{1,3,2,0:T(8,128)S(1)} fusion(f32[4,256,256]{2,1,0:T(8,128)S(1)} %fusion.39, f32[4,4,256]{2,0,1:T(4,128)S(1)} %get-tuple-element.169, pred[4,256,256]{2,1,0:T(8,128)(4,1)} %compare_and_fusion, f32[4,256,4,64]{1,0,3,2:T(4,128)} %get-tuple-element.157), kind=kOutput, calls=%fused_computation.25 | convolution fusion | flops 809500672 | bytes 3424256 | tf_op jit(solution)/shard_map/hcts,cshp->cthp/dot_general | solution.py:111
  36.4 26.1 %while.27 = (s32[]{:T(128)}, f32[4,64,256]{2,1,0:T(8,128)S(1)}, f32[4]{0:T(128)S(1)}, f32[4,64,256]{2,1,0:T(8,128)S(1)}, s32[]{:T(128)}) while((s32[]{:T(128)}, f32[4,64,256]{2,1,0:T(8,128)S(1)}, f32[4]{0:T(128)S(1)}, f32[4,64,256]{2,1,0:T(8,128)S(1)}, s32[]{:T(128)}) %tuple.61), condition=%wide.region_10.11_spmd, body=%wide.region_9.10_spmd.sunk | while | flops 131074 | bytes 1835125 | solution.py:140
  36.5 0.1 multiply_add_fusion.2
  36.6 3.5 %collective-permute-start = (f32[4,64,256]{2,1,0:T(8,128)S(1)}, f32[4,64,256]{2,1,0:T(8,128)S(1)}, u32[]{:S(2)}, u32[]{:S(2)}) collective-permute-start(f32[4,64,256]{2,1,0:T(8,128)S(1)} %multiply_add_fusion.2), channel_id=1, source_target_pairs={{0,8},{8,16},{16,24},{1,9},{9,17},{17,25},{2,10},{10,18},{18,26},{... | collective-permute-start | bytes 786440 | tf_op jit(solution)/shard_map/while/body/eval_jaxpr/ppermute | solution.py:20
  40.1 5.2 %collective-permute-done = f32[4,64,256]{2,1,0:T(8,128)S(1)} collective-permute-done((f32[4,64,256]{2,1,0:T(8,128)S(1)}, f32[4,64,256]{2,1,0:T(8,128)S(1)}, u32[]{:S(2)}, u32[]{:S(2)}) %collective-permute-start) | collective-permute-done | bytes 262176 | tf_op jit(solution)/shard_map/while/body/eval_jaxpr/ppermute | solution.py:20
  45.3 0.1 multiply_add_fusion.2
  45.4 4.4 %collective-permute-start = (f32[4,64,256]{2,1,0:T(8,128)S(1)}, f32[4,64,256]{2,1,0:T(8,128)S(1)}, u32[]{:S(2)}, u32[]{:S(2)}) collective-permute-start(f32[4,64,256]{2,1,0:T(8,128)S(1)} %multiply_add_fusion.2), channel_id=1, source_target_pairs={{0,8},{8,16},{16,24},{1,9},{9,17},{17,25},{2,10},{10,18},{18,26},{... | collective-permute-start | bytes 786440 | tf_op jit(solution)/shard_map/while/body/eval_jaxpr/ppermute | solution.py:20
  49.8 4.3 %collective-permute-done = f32[4,64,256]{2,1,0:T(8,128)S(1)} collective-permute-done((f32[4,64,256]{2,1,0:T(8,128)S(1)}, f32[4,64,256]{2,1,0:T(8,128)S(1)}, u32[]{:S(2)}, u32[]{:S(2)}) %collective-permute-start) | collective-permute-done | bytes 262176 | tf_op jit(solution)/shard_map/while/body/eval_jaxpr/ppermute | solution.py:20
  54.2 0.1 multiply_add_fusion.2
  54.2 4.4 %collective-permute-start = (f32[4,64,256]{2,1,0:T(8,128)S(1)}, f32[4,64,256]{2,1,0:T(8,128)S(1)}, u32[]{:S(2)}, u32[]{:S(2)}) collective-permute-start(f32[4,64,256]{2,1,0:T(8,128)S(1)} %multiply_add_fusion.2), channel_id=1, source_target_pairs={{0,8},{8,16},{16,24},{1,9},{9,17},{17,25},{2,10},{10,18},{18,26},{... | collective-permute-start | bytes 786440 | tf_op jit(solution)/shard_map/while/body/eval_jaxpr/ppermute | solution.py:20
  58.7 3.9 %collective-permute-done = f32[4,64,256]{2,1,0:T(8,128)S(1)} collective-permute-done((f32[4,64,256]{2,1,0:T(8,128)S(1)}, f32[4,64,256]{2,1,0:T(8,128)S(1)}, u32[]{:S(2)}, u32[]{:S(2)}) %collective-permute-start) | collective-permute-done | bytes 262176 | tf_op jit(solution)/shard_map/while/body/eval_jaxpr/ppermute | solution.py:20
  62.5 2.1 %fusion.15 = f32[4,256,4,64]{1,3,2,0:T(8,128)S(1)} fusion(f32[4,256,4,64]{1,3,2,0:T(8,128)S(1)} %fusion.16, bf16[4,256,256,1]{2,1,3,0:T(8,128)(2,1)S(1)} %bitcast.59, f32[4,256,4,64]{1,0,3,2:T(4,128)S(1)} %reshape.183, f32[4,4,64,256]{3,2,1,0:T(8,128)} %get-tuple-element.67, f32[4]{0:T(128)S(1)} %copy-done.8, f32[4,256,4]{1,2,0:T(4,128)S(1)} %get-tuple-element.168, ...), kind=kOutput, calls=%fused_computation.24 | convolution fusion | flops 806879232 | bytes 4997200 | tf_op jit(solution)/shard_map/ctn,chpn->cthp/dot_general | solution.py:144
  64.7 0.7 copy.79
  65.4 0.2 copy.86
  65.6 0.1 copy-done
  65.7 0.4 multiply_reduce_fusion
  66.1 11.8 %psum.7 = f32[1024]{0:T(1024)S(1)} all-reduce(f32[1024]{0:T(1024)S(1)} %multiply_reduce_fusion), channel_id=1, replica_groups=mesh['context'=4,'head'=8] {'head'}, use_global_device_ids=true, to_apply=%region_12.13 | all-reduce | flops 1024 | bytes 8192 | tf_op jit(solution)/shard_map/psum | solution.py:151
  77.9 0.4 multiply_convert_fusion.1
  78.3 1.0 %copy.81 = bf16[1024,256]{1,0:T(8,128)(2,1)} copy(bf16[1024,256]{0,1:T(8,128)(2,1)S(1)} %multiply_convert_fusion.1) | data formatting | bytes 1048576 | tf_op jit(solution)/shard_map/convert_element_type | solution.py:154
  (59 shorter events, 0.8 us)
Async XLA Ops:
  0.0 7.6 %copy-start.9 = (s32[16]{0:T(128)S(1)}, s32[16]{0:T(128)}, u32[]{:S(2)}) copy-start(s32[16]{0:T(128)} %param.29) | copy-start | bytes 196
  0.0 8.9 %copy-start.4 = (f32[4,256]{1,0:T(4,128)S(1)}, f32[4,256]{1,0:T(4,128)}, u32[]{:S(2)}) copy-start(f32[4,256]{1,0:T(4,128)} %param.21) | copy-start | bytes 12292
  0.0 11.4 %copy-start.10 = (f32[4]{0:T(128)S(1)}, f32[4]{0:T(128)}, u32[]{:S(2)}) copy-start(f32[4]{0:T(128)} %param.26) | copy-start | bytes 52
  0.0 11.4 %copy-start.7 = (f32[4]{0:T(128)S(1)}, f32[4]{0:T(128)}, u32[]{:S(2)}) copy-start(f32[4]{0:T(128)} %param.25) | copy-start | bytes 52
  0.0 11.4 %copy-start.3 = (bf16[4,1024]{1,0:T(4,128)(2,1)S(1)}, bf16[4,1024]{1,0:T(4,128)(2,1)}, u32[]{:S(2)}) copy-start(bf16[4,1024]{1,0:T(4,128)(2,1)} %param.20) | copy-start | bytes 24580
  0.0 18.6 %copy-start.6 = (f32[256]{0:T(256)S(1)}, f32[256]{0:T(256)}, u32[]{:S(2)}) copy-start(f32[256]{0:T(256)} %param.22) | copy-start | bytes 3076
  0.1 18.7 %copy-start.2 = (bf16[1024,256]{1,0:T(8,128)(2,1)S(1)}, bf16[1024,256]{1,0:T(8,128)(2,1)}, u32[]{:S(2)}) copy-start(bf16[1024,256]{1,0:T(8,128)(2,1)} %param.19) | copy-start | bytes 1572868
  1.4 18.4 %copy-start.1 = (bf16[1024,256]{1,0:T(8,128)(2,1)S(1)}, bf16[1024,256]{1,0:T(8,128)(2,1)}, u32[]{:S(2)}) copy-start(bf16[1024,256]{1,0:T(8,128)(2,1)} %param.17) | copy-start | bytes 1572868
  2.6 17.1 %collective-permute-start.1 = (bf16[3,768]{1,0:T(4,128)(2,1)S(1)}, bf16[3,768]{1,0:T(4,128)(2,1)S(1)}, u32[]{:S(2)}, u32[]{:S(2)}) collective-permute-start(bf16[3,768]{1,0:T(4,128)(2,1)S(1)} %slice.96), channel_id=1, source_target_pairs={{0,8},{8,16},{16,24},{1,9},{9,17},{17,25},{2,10},{10,18},{18,26},{... | collective-permute-start | bytes 13832 | tf_op jit(solution)/shard_map/ppermute | solution.py:20
  36.4 26.1 %copy-start.8 = (f32[4]{0:T(128)S(1)}, f32[4]{0:T(128)}, u32[]{:S(2)}) copy-start(f32[4]{0:T(128)} %param.27) | copy-start | bytes 52
  36.6 8.8 %collective-permute-start = (f32[4,64,256]{2,1,0:T(8,128)S(1)}, f32[4,64,256]{2,1,0:T(8,128)S(1)}, u32[]{:S(2)}, u32[]{:S(2)}) collective-permute-start(f32[4,64,256]{2,1,0:T(8,128)S(1)} %multiply_add_fusion.2), channel_id=1, source_target_pairs={{0,8},{8,16},{16,24},{1,9},{9,17},{17,25},{2,10},{10,18},{18,26},{... | collective-permute-start | bytes 786440 | tf_op jit(solution)/shard_map/while/body/eval_jaxpr/ppermute | solution.py:20
  45.4 8.7 %collective-permute-start = (f32[4,64,256]{2,1,0:T(8,128)S(1)}, f32[4,64,256]{2,1,0:T(8,128)S(1)}, u32[]{:S(2)}, u32[]{:S(2)}) collective-permute-start(f32[4,64,256]{2,1,0:T(8,128)S(1)} %multiply_add_fusion.2), channel_id=1, source_target_pairs={{0,8},{8,16},{16,24},{1,9},{9,17},{17,25},{2,10},{10,18},{18,26},{... | collective-permute-start | bytes 786440 | tf_op jit(solution)/shard_map/while/body/eval_jaxpr/ppermute | solution.py:20
  54.2 8.3 %collective-permute-start = (f32[4,64,256]{2,1,0:T(8,128)S(1)}, f32[4,64,256]{2,1,0:T(8,128)S(1)}, u32[]{:S(2)}, u32[]{:S(2)}) collective-permute-start(f32[4,64,256]{2,1,0:T(8,128)S(1)} %multiply_add_fusion.2), channel_id=1, source_target_pairs={{0,8},{8,16},{16,24},{1,9},{9,17},{17,25},{2,10},{10,18},{18,26},{... | collective-permute-start | bytes 786440 | tf_op jit(solution)/shard_map/while/body/eval_jaxpr/ppermute | solution.py:20
  64.7 1.0 %copy-start = (bf16[1024,256]{0,1:T(8,128)(2,1)S(1)}, bf16[1024,256]{0,1:T(8,128)(2,1)}, u32[]{:S(2)}) copy-start(bf16[1024,256]{0,1:T(8,128)(2,1)} %copy.80) | copy-start | bytes 1572868
  64.7 13.2 %copy-start.5 = (f32[256]{0:T(256)S(1)}, f32[256]{0:T(256)}, u32[]{:S(2)}) copy-start(f32[256]{0:T(256)} %param.28) | copy-start | bytes 3076
where the time goes:
time: 79.7 us; the launch traced here: 79.3 us
  other arithmetic  18.4 us (23%)
  starting transfers between devices  17.2 us (22%)
  waiting for transfers between devices  13.4 us (17%)
  blocking collectives  11.8 us (15%)
  matrix products  9.54 us (12%)
  local copies, waits for them, and re-layouts  8.32 us (10%)
    ppermute x4, starting transfers between devices, from_behind(): return lax.ppermute(shard, axis, pairs)  17.2 us
    ppermute x4, waiting for transfers between devices, from_behind(): return lax.ppermute(shard, axis, pairs)  13.4 us
    psum x1, blocking collectives, shards(): total_squares = lax.psum(squares, 'head')  11.8 us
    dot_general x1, matrix products, shards(): jnp.einsum('hcts,cshp->cthp', mixing, weighted, precision=exact_mode)  6.35 us
    another operation x8, other arithmetic  6.34 us
    convert_element_type x1, other arithmetic, conv_silu(): return jax.nn.silu(summed).astype(jnp.bfloat16)  2.97 us
    dynamic_update_slice x4, other arithmetic, shards(): lax.scan(advance, (zero_state, unit_decay), (summaries, carry_decay))  2.94 us
    dot_general x1, matrix products, shards(): jnp.einsum('ctn,chpn->cthp', c_vals, incoming, precision=exact_mode)  2.15 us
  transfers between devices with their start and end apart: 4, of which 3 were waited for; matrix products, arithmetic and copies ran while one was open for 15% of the time, Pallas kernels for 0%

commit v1 on v0

v1 whole, which is shorter than its diff:
```python
import functools
import math

import jax
import jax.numpy as jnp
from jax import lax
from jax.experimental import pallas as pl
from jax.experimental.pallas import tpu as pltpu
from jax.sharding import PartitionSpec as P

HEAD_DIM = 64
STATE = 256
GROUPS = 8
CONV = 4
BLOCK = 256
TILE = 128
HALO = 16
CHUNKS = 4
LOG2E = math.log2(math.e)
NORM_FLOOR = 1e-05
F32 = jnp.float32
BF16 = jnp.bfloat16


def dot(a, b, dims):
    return lax.dot_general(a, b, (dims, ((), ())), preferred_element_type=F32)


def silu_half(h):
    return h + h * jnp.tanh(h)


def split_rows(v, parts):
    pieces = []
    for _ in range(parts):
        piece = v.astype(BF16).astype(F32)
        pieces.append(piece)
        v = v - piece
    return jnp.concatenate(pieces, axis=0).astype(BF16)


def layer_kernel(
    n_ctx,
    n_head,
    x_hbm,
    bc_hbm,
    z_hbm,
    dt_ref,
    xw_ref,
    xb_ref,
    bcw_ref,
    bcb_ref,
    dt_bias,
    a_log,
    skip_gain,
    nw_ref,
    doc_len,
    out_hbm,
    ext,
    z_buf,
    mixed,
    tail_buf,
    entry_buf,
    state_buf,
    end_buf,
    y_buf,
    gate_buf,
    send_buf,
    recv_buf,
    sums,
    out_buf,
    load_sems,
    halo_send,
    halo_recv,
    state_send,
    state_recv,
    sums_send,
    sums_recv,
    out_sems,
):
    rows = x_hbm.shape[0]
    width = x_hbm.shape[1]
    heads = dt_ref.shape[0]
    docs = doc_len.shape[0]
    blocks = rows // BLOCK
    tiles = rows // TILE
    ctx = lax.axis_index("context")
    me = lax.axis_index("head")
    per_group = n_head * heads // GROUPS
    group = me * heads // per_group
    b_at = pl.multiple_of(group * STATE, STATE)
    c_at = pl.multiple_of((GROUPS + group) * STATE, STATE)
    not_last = ctx < n_ctx - 1

    barrier = pltpu.get_barrier_semaphore()

    @pl.when(ctx > 0)
    def _():
        pl.semaphore_signal(
            barrier, inc=1, device_id=(ctx - 1, me), device_id_type=pl.DeviceIdType.MESH
        )

    peers = [lax.rem(me + d, n_head) for d in range(1, n_head)]
    for peer in peers:
        pl.semaphore_signal(
            barrier, inc=1, device_id=(ctx, peer), device_id_type=pl.DeviceIdType.MESH
        )

    own = pl.ds(HALO, rows)
    loads = [
        pltpu.make_async_copy(x_hbm, ext.at[own, pl.ds(0, width)], load_sems.at[0]),
        pltpu.make_async_copy(
            bc_hbm.at[:, pl.ds(b_at, STATE)], ext.at[own, pl.ds(width, STATE)], load_sems.at[1]
        ),
        pltpu.make_async_copy(
            bc_hbm.at[:, pl.ds(c_at, STATE)],
            ext.at[own, pl.ds(width + STATE, STATE)],
            load_sems.at[2],
        ),
        pltpu.make_async_copy(z_hbm, z_buf, load_sems.at[3]),
    ]
    for load in loads:
        load.start()

    @pl.when(ctx == 0)
    def _():
        ext[pl.ds(0, HALO), :] = jnp.zeros((HALO, width + 2 * STATE), BF16)
        recv_buf[...] = jnp.zeros((STATE, width), BF16)

    pl.semaphore_wait(barrier, n_head - 1 + jnp.where(not_last, 1, 0))

    right = (jnp.minimum(ctx + 1, n_ctx - 1), me)
    last_rows = pl.ds(rows - HALO, HALO)
    halo_src = [
        x_hbm.at[last_rows, :],
        bc_hbm.at[last_rows, pl.ds(b_at, STATE)],
        bc_hbm.at[last_rows, pl.ds(c_at, STATE)],
    ]
    halo_at = [pl.ds(0, width), pl.ds(width, STATE), pl.ds(width + STATE, STATE)]

    def halo_copy(i):
        return pltpu.make_async_remote_copy(
            src_ref=halo_src[i],
            dst_ref=ext.at[pl.ds(0, HALO), halo_at[i]],
            send_sem=halo_send.at[i],
            recv_sem=halo_recv.at[i],
            device_id=right,
            device_id_type=pl.DeviceIdType.MESH,
        )

    @pl.when(not_last)
    def _():
        for i in range(3):
            halo_copy(i).start()

    first = ctx * rows
    ends, begins, total = [], [], jnp.int32(0)
    for d in range(docs):
        begins.append(total)
        total = total + doc_len[d]
        ends.append(total)

    def tokens_left(pos):
        end = jnp.zeros_like(pos)
        for d in reversed(range(docs)):
            end = jnp.where(pos < ends[d], ends[d], end)
        return jnp.where(pos < 0, -1, end - 1 - pos)

    ext_lanes = rows + TILE
    left_ext = tokens_left(first - HALO + lax.broadcasted_iota(jnp.int32, (1, ext_lanes), 1))
    lane = lax.broadcasted_iota(jnp.int32, (1, rows), 1)
    pos = first + lane
    left = tokens_left(pos)
    begin = jnp.zeros_like(pos)
    for d in range(docs):
        begin = jnp.where(pos >= begins[d], begins[d], begin)
    lane_b = lax.rem(lane, BLOCK)
    alive = pos - begin > lane_b
    tail_same = left >= BLOCK - 1 - lane_b

    head_row = lax.broadcasted_iota(jnp.int32, (heads, rows), 0)
    bias_col = jnp.zeros((heads, rows), F32)
    alog_col = jnp.zeros((heads, rows), F32)
    for h in range(heads):
        bias_col = jnp.where(head_row == h, dt_bias[h], bias_col)
        alog_col = jnp.where(head_row == h, a_log[h], alog_col)
    raw = dt_ref[...].astype(F32) + bias_col
    step = jnp.maximum(raw, 0.0) + jnp.log1p(jnp.exp(-jnp.abs(raw)))
    log_decay = step * (jnp.exp(alog_col) * (-LOG2E))
    per_block = jnp.concatenate(
        [log_decay[:, c * BLOCK : (c + 1) * BLOCK] for c in range(blocks)], axis=0
    )
    upper = (
        lax.broadcasted_iota(jnp.int32, (BLOCK, BLOCK), 0)
        <= lax.broadcasted_iota(jnp.int32, (BLOCK, BLOCK), 1)
    )
    n_run = blocks * heads
    summed = dot(split_rows(per_block, 3), upper.astype(F32).astype(BF16), ((1,), (0,)))
    run = summed[:n_run] + summed[n_run : 2 * n_run] + summed[2 * n_run :]
    run_col = jnp.transpose(run)
    ends_run = run[:, BLOCK - 1 : BLOCK]
    running = jnp.concatenate([run[c * heads : (c + 1) * heads] for c in range(blocks)], axis=1)
    to_end = jnp.concatenate(
        [
            ends_run[c * heads : (c + 1) * heads] - run[c * heads : (c + 1) * heads]
            for c in range(blocks)
        ],
        axis=1,
    )
    tail_rows = jnp.where(tail_same, jnp.exp2(to_end), 0.0) * step
    entry_rows = jnp.where(alive, jnp.exp2(running), 0.0)

    spread = (
        lax.broadcasted_iota(jnp.int32, (heads, width), 0)
        == lax.broadcasted_iota(jnp.int32, (heads, width), 1) // HEAD_DIM
    ).astype(F32)
    spread2 = jnp.concatenate([spread, spread], axis=0).astype(BF16)
    tail_buf[...] = dot(split_rows(tail_rows, 2), spread2, ((0,), (0,)))
    entry_buf[...] = dot(split_rows(entry_rows, 2), spread2, ((0,), (0,)))

    decay_rows = []
    for c in range(blocks):
        at = c * BLOCK + BLOCK - 1
        decay_rows.append(jnp.sum(entry_rows[:, at : at + 1] * spread, axis=0, keepdims=True))
    skip_row = jnp.zeros((1, width), F32)
    head_lane = lax.broadcasted_iota(jnp.int32, (1, width), 1) // HEAD_DIM
    for h in range(heads):
        skip_row = jnp.where(head_lane == h, skip_gain[h], skip_row)

    reach = TILE + HALO
    offset = lax.broadcasted_iota(jnp.int32, (TILE, reach), 1) - lax.broadcasted_iota(
        jnp.int32, (TILE, reach), 0
    )
    bands = [jnp.where(offset == HALO - j, 1.0, 0.0).astype(F32) for j in range(1, CONV)]
    taps = [xw_ref[...] * 0.5] + [
        bcw_ref[:, pl.ds(at, STATE)] * 0.5 for at in (b_at, c_at)
    ]
    conv_bias = [xb_ref[...] * 0.5] + [bcb_ref[:, pl.ds(at, STATE)] * 0.5 for at in (b_at, c_at)]
    part_at = [(0, width), (width, STATE), (width + STATE, STATE)]

    def conv_tile(i, parts):
        at = i * TILE
        ok = left_ext[:, at : at + reach]
        shift = jnp.concatenate(
            [jnp.where(ok >= j, bands[j - 1], 0.0) for j in range(1, CONV)], axis=0
        ).astype(BF16)
        for part in parts:
            begin_at, size = part_at[part]
            source = ext[at : at + reach, begin_at : begin_at + size]
            moved = dot(shift, source, ((1,), (0,)))
            h = conv_bias[part] + taps[part][3:4] * source[HALO:].astype(F32)
            h = h + taps[part][2:3] * moved[:TILE]
            h = h + taps[part][1:2] * moved[TILE : 2 * TILE]
            h = h + taps[part][0:1] * moved[2 * TILE :]
            mixed[at : at + TILE, begin_at : begin_at + size] = silu_half(h).astype(BF16)

    loads[0].wait()
    loads[1].wait()
    for i in range(1, tiles):
        conv_tile(i, (0, 1))

    @pl.when(ctx > 0)
    def _():
        for i in range(3):
            halo_copy(i).wait_recv()

    conv_tile(0, (0, 1))

    state = jnp.zeros((STATE, width), F32)
    for c in range(blocks):
        at = c * BLOCK
        state_buf[c] = state
        x_tail = (mixed[at : at + BLOCK, :width].astype(F32) * tail_buf[at : at + BLOCK, :]).astype(
            BF16
        )
        summary = dot(mixed[at : at + BLOCK, width : width + STATE], x_tail, ((0,), (0,)))
        state = state * decay_rows[c] + summary
    end_buf[...] = state
    shard_decay = decay_rows[0]
    for c in range(1, blocks):
        shard_decay = shard_decay * decay_rows[c]

    chunk = STATE // CHUNKS

    def state_copy(i):
        at = pl.ds(i * chunk, chunk)
        return pltpu.make_async_remote_copy(
            src_ref=send_buf.at[at, :],
            dst_ref=recv_buf.at[at, :],
            send_sem=state_send.at[i],
            recv_sem=state_recv.at[i],
            device_id=right,
            device_id_type=pl.DeviceIdType.MESH,
        )

    @pl.when(ctx == 0)
    def _():
        for i in range(CHUNKS):
            at = pl.ds(i * chunk, chunk)
            send_buf[at, :] = end_buf[at, :].astype(BF16)
            state_copy(i).start()

    def forward(stage):
        mine = ctx == stage if stage < blocks else ctx >= stage

        @pl.when(mine & not_last)
        def _():
            for i in range(CHUNKS):
                at = pl.ds(i * chunk, chunk)
                state_copy(i).wait_recv()
                send_buf[at, :] = (
                    end_buf[at, :] + shard_decay * recv_buf[at, :].astype(F32)
                ).astype(BF16)
                state_copy(i).start()

    loads[2].wait()
    loads[3].wait()
    gap_at = lax.broadcasted_iota(jnp.int32, (BLOCK, BLOCK), 0) - lax.broadcasted_iota(
        jnp.int32, (BLOCK, BLOCK), 1
    )
    for c in range(blocks):
        at = c * BLOCK
        for i in range(BLOCK // TILE):
            conv_tile(c * (BLOCK // TILE) + i, (2,))
        x_c = mixed[at : at + BLOCK, :width]
        b_c = mixed[at : at + BLOCK, width : width + STATE]
        c_c = mixed[at : at + BLOCK, width + STATE :]
        inner = dot(c_c, b_c, ((1,), (1,)))
        inner = jnp.where((gap_at >= 0) & (gap_at <= left[:, at : at + BLOCK]), inner, 0.0)
        y = skip_row * x_c.astype(F32)
        for h in range(heads):
            r = c * heads + h
            gap = jnp.minimum(run_col[:, r : r + 1] - run[r : r + 1], 0.0)
            mix = jnp.exp2(gap) * inner * step[h : h + 1, at : at + BLOCK]
            x_h = x_c * (head_lane == h).astype(F32).astype(BF16)
            y = y + dot(mix.astype(BF16), x_h, ((1,), (0,)))
        y_buf[at : at + BLOCK, :] = y
        gate_buf[at : at + BLOCK, :] = silu_half(z_buf[at : at + BLOCK, :].astype(F32) * 0.5)
        forward(c + 1)

    @pl.when(ctx == n_ctx - 1)
    def _():
        for i in range(CHUNKS):
            state_copy(i).wait_recv()

    entering = recv_buf[...].astype(F32)
    so_far = jnp.ones((1, width), F32)
    ones = jnp.ones((8, width), BF16)
    slot_row = lax.broadcasted_iota(jnp.int32, (tiles, TILE), 0)
    squares = jnp.zeros((tiles, TILE), F32)
    for c in range(blocks):
        at = c * BLOCK
        incoming = (state_buf[c] + so_far * entering).astype(BF16)
        so_far = so_far * decay_rows[c]
        from_state = dot(mixed[at : at + BLOCK, width + STATE :], incoming, ((1,), (0,)))
        y = y_buf[at : at + BLOCK, :] + entry_buf[at : at + BLOCK, :] * from_state
        gated = y * gate_buf[at : at + BLOCK, :]
        y_buf[at : at + BLOCK, :] = gated
        row = dot(ones, (gated * gated).astype(BF16), ((1,), (1,)))
        for i in range(BLOCK // TILE):
            squares = jnp.where(
                slot_row == c * (BLOCK // TILE) + i, row[0:1, i * TILE : (i + 1) * TILE], squares
            )
    sums[me] = squares

    def sums_copy(d):
        return pltpu.make_async_remote_copy(
            src_ref=sums.at[me],
            dst_ref=sums.at[me],
            send_sem=sums_send.at[d],
            recv_sem=sums_recv.at[d],
            device_id=(ctx, peers[d]),
            device_id_type=pl.DeviceIdType.MESH,
        )

    for d in range(n_head - 1):
        sums_copy(d).start()
    for d in range(n_head - 1):
        sums_copy(d).wait_recv()
    every = sums[0]
    for d in range(1, n_head):
        every = every + sums[d]
    scale = lax.rsqrt(every / (n_head * width) + NORM_FLOOR)
    norm_row = nw_ref[...]
    stores = []
    for c in range(blocks):
        at = c * BLOCK
        for i in range(BLOCK // TILE):
            t = c * (BLOCK // TILE) + i
            column = jnp.transpose(jnp.broadcast_to(scale[t : t + 1, :], (TILE, TILE)))
            column = jnp.concatenate([column] * (width // TILE), axis=1)
            piece = y_buf[t * TILE : (t + 1) * TILE, :] * column * norm_row
            out_buf[t * TILE : (t + 1) * TILE, :] = piece.astype(BF16)
        store = pltpu.make_async_copy(
            out_buf.at[pl.ds(at, BLOCK), :], out_hbm.at[pl.ds(at, BLOCK), :], out_sems.at[c]
        )
        store.start()
        stores.append(store)

    for d in range(n_head - 1):
        sums_copy(d).wait_send()

    @pl.when(not_last)
    def _():
        for i in range(3):
            halo_copy(i).wait_send()
        for i in range(CHUNKS):
            state_copy(i).wait_send()

    for store in stores:
        store.wait()


def shards(
    x_in,
    bc_in,
    z_in,
    dt_in,
    conv_x_w,
    conv_x_b,
    conv_bc_w,
    conv_bc_b,
    dt_bias,
    a_log,
    skip_gain,
    norm_w,
    doc_len,
):
    rows, width = x_in.shape
    n_ctx = lax.axis_size("context")
    n_head = lax.axis_size("head")
    blocks = rows // BLOCK
    tiles = rows // TILE
    anywhere = pl.BlockSpec(memory_space=pltpu.HBM)
    vmem = pl.BlockSpec(memory_space=pltpu.VMEM)
    smem = pl.BlockSpec(memory_space=pltpu.SMEM)
    dma = pltpu.SemaphoreType.DMA
    return pl.pallas_call(
        functools.partial(layer_kernel, n_ctx, n_head),
        out_shape=jax.ShapeDtypeStruct((rows, width), BF16),
        in_specs=[anywhere] * 3 + [vmem] * 5 + [smem] * 3 + [vmem, smem],
        out_specs=anywhere,
        scratch_shapes=[
            pltpu.VMEM((rows + HALO, width + 2 * STATE), BF16),
            pltpu.VMEM((rows, width), BF16),
            pltpu.VMEM((rows, width + 2 * STATE), BF16),
            pltpu.VMEM((rows, width), F32),
            pltpu.VMEM((rows, width), F32),
            pltpu.VMEM((blocks, STATE, width), F32),
            pltpu.VMEM((STATE, width), F32),
            pltpu.VMEM((rows, width), F32),
            pltpu.VMEM((rows, width), F32),
            pltpu.VMEM((STATE, width), BF16),
            pltpu.VMEM((STATE, width), BF16),
            pltpu.VMEM((n_head, tiles, TILE), F32),
            pltpu.VMEM((rows, width), BF16),
            dma((4,)),
            dma((3,)),
            dma((3,)),
            dma((CHUNKS,)),
            dma((CHUNKS,)),
            dma((n_head - 1,)),
            dma((n_head - 1,)),
            dma((blocks,)),
        ],
        compiler_params=pltpu.CompilerParams(
            collective_id=0, has_side_effects=True, vmem_limit_bytes=40 * 1024 * 1024
        ),
    )(
        x_in,
        bc_in,
        z_in,
        dt_in,
        conv_x_w,
        conv_x_b.reshape(1, -1),
        conv_bc_w,
        conv_bc_b.reshape(1, -1),
        dt_bias,
        a_log,
        skip_gain,
        norm_w.reshape(1, -1),
        doc_len,
    )


def solution(mesh):
    return jax.shard_map(
        shards,
        mesh=mesh,
        in_specs=(
            P("context", "head"),
            P("context", None),
            P("context", "head"),
            P("head", "context"),
            P(None, "head"),
            P("head"),
            P(),
            P(),
            P("head"),
            P("head"),
            P("head"),
            P("head"),
            P(),
        ),
        out_specs=P("context", "head"),
        check_vma=False,
    )
```

time: 79.7 us -> 33.4 us (0.42)
  the two profiles are of different devices: /device:TPU:0 before, /device:TPU:25 now
where the time goes in v1:
time: 33.4 us; the launch traced here: 32.9 us
  Pallas kernels  19.7 us (59%)
  local copies, waits for them, and re-layouts  13.2 us (40%)
    pallas_call x1, Pallas kernels, shards(): pl.pallas_call(functools.partial(layer_kernel, n_ctx, n_head), out_shape=...  19.7 us
    unnamed x27, local copies, waits for them, and re-layouts  13.2 us

profile of v1, /device:TPU:25, one launch (start us, length us, event | category | flops | bytes accessed | tf_op | source)
XLA Modules:
  0.0 32.9 jit_solution(6823933024989127227)
XLA Ops:
  0.0 0.0 copy-start
  0.0 3.4 %copy-done = bf16[1024,4096]{1,0:T(8,128)(2,1)S(1)} copy-done((bf16[1024,4096]{1,0:T(8,128)(2,1)S(1)}, bf16[1024,4096]{1,0:T(8,128)(2,1)}, u32[]{:S(2)}) %copy-start) | copy-done | bytes 8388632
  3.4 0.0 copy-start.1
  3.4 1.0 %copy-done.1 = bf16[1024,256]{1,0:T(8,128)(2,1)S(1)} copy-done((bf16[1024,256]{1,0:T(8,128)(2,1)S(1)}, bf16[1024,256]{1,0:T(8,128)(2,1)}, u32[]{:S(2)}) %copy-start.1) | copy-done | bytes 524312
  4.4 0.0 copy-start.2
  4.4 1.0 %copy-done.2 = bf16[1024,256]{1,0:T(8,128)(2,1)S(1)} copy-done((bf16[1024,256]{1,0:T(8,128)(2,1)S(1)}, bf16[1024,256]{1,0:T(8,128)(2,1)}, u32[]{:S(2)}) %copy-start.2) | copy-done | bytes 524312
  5.5 0.0 copy-start.3
  5.5 0.8 %copy-done.3 = f32[4,4096]{1,0:T(4,128)S(1)} copy-done((f32[4,4096]{1,0:T(4,128)S(1)}, f32[4,4096]{1,0:T(4,128)}, u32[]{:S(2)}) %copy-start.3) | copy-done | bytes 65560
  6.3 0.0 copy-start.4
  6.3 0.7 %copy-done.4 = f32[4096]{0:T(1024)S(1)} copy-done((f32[4096]{0:T(1024)S(1)}, f32[4096]{0:T(1024)}, u32[]{:S(2)}) %copy-start.4) | copy-done | bytes 16408
  7.0 0.0 copy-start.5
  7.0 0.7 %copy-done.5 = bf16[4,1024]{1,0:T(4,128)(2,1)S(1)} copy-done((bf16[4,1024]{1,0:T(4,128)(2,1)S(1)}, bf16[4,1024]{1,0:T(4,128)(2,1)}, u32[]{:S(2)}) %copy-start.5) | copy-done | bytes 8216
  7.7 0.0 copy-start.6
  7.7 0.7 %copy-done.6 = f32[4,256]{1,0:T(4,128)S(1)} copy-done((f32[4,256]{1,0:T(4,128)S(1)}, f32[4,256]{1,0:T(4,128)}, u32[]{:S(2)}) %copy-start.6) | copy-done | bytes 4120
  8.4 0.0 copy-start.7
  8.4 0.7 %copy-done.7 = f32[256]{0:T(256)S(1)} copy-done((f32[256]{0:T(256)S(1)}, f32[256]{0:T(256)}, u32[]{:S(2)}) %copy-start.7) | copy-done | bytes 1048
  9.1 0.0 copy-start.8
  9.1 0.7 %copy-done.8 = f32[256]{0:T(256)S(1)} copy-done((f32[256]{0:T(256)S(1)}, f32[256]{0:T(256)}, u32[]{:S(2)}) %copy-start.8) | copy-done | bytes 1048
  9.8 0.0 copy-start.9
  9.8 0.7 %copy-done.9 = f32[4]{0:T(128)S(1)} copy-done((f32[4]{0:T(128)S(1)}, f32[4]{0:T(128)}, u32[]{:S(2)}) %copy-start.9) | copy-done | bytes 40
  10.4 0.0 copy-start.10
  10.4 0.7 %copy-done.10 = f32[4]{0:T(128)S(1)} copy-done((f32[4]{0:T(128)S(1)}, f32[4]{0:T(128)}, u32[]{:S(2)}) %copy-start.10) | copy-done | bytes 40
  11.1 0.0 copy-start.11
  11.1 0.7 %copy-done.11 = f32[4]{0:T(128)S(1)} copy-done((f32[4]{0:T(128)S(1)}, f32[4]{0:T(128)}, u32[]{:S(2)}) %copy-start.11) | copy-done | bytes 40
  11.7 0.0 copy-start.12
  11.7 0.7 %copy-done.12 = s32[16]{0:T(128)S(1)} copy-done((s32[16]{0:T(128)S(1)}, s32[16]{0:T(128)}, u32[]{:S(2)}) %copy-start.12) | copy-done | bytes 88
  12.4 19.7 %shard_map.127 = bf16[1024,256]{1,0:T(8,128)(2,1)S(1)} custom-call(bf16[1024,256]{1,0:T(8,128)(2,1)S(1)} %copy-done.1, bf16[1024,4096]{1,0:T(8,128)(2,1)S(1)} %copy-done, bf16[1024,256]{1,0:T(8,128)(2,1)S(1)} %copy-done.2, bf16[4,1024]{1,0:T(4,128)(2,1)S(1)} %copy-done.5, f32[4,256]{1,0:T(4,128)S(1)} %copy-done.6, f32[1,256]{1,0:T(1,128)S(1)} %bitcast.4, ...), custom_call_target="tpu_custom_call" | custom-call | tf_op jit(solution)/shard_map/pallas_call | solution.py:438
  32.1 0.8 %copy.15 = bf16[1024,256]{1,0:T(8,128)(2,1)} copy(bf16[1024,256]{1,0:T(8,128)(2,1)S(1)} %shard_map.127) | data formatting | bytes 1048576
Async XLA Ops:
  0.0 3.4 %copy-start = (bf16[1024,4096]{1,0:T(8,128)(2,1)S(1)}, bf16[1024,4096]{1,0:T(8,128)(2,1)}, u32[]{:S(2)}) copy-start(bf16[1024,4096]{1,0:T(8,128)(2,1)} %bc_hbm.1) | copy-start | bytes 25165828
  3.4 1.0 %copy-start.1 = (bf16[1024,256]{1,0:T(8,128)(2,1)S(1)}, bf16[1024,256]{1,0:T(8,128)(2,1)}, u32[]{:S(2)}) copy-start(bf16[1024,256]{1,0:T(8,128)(2,1)} %x_hbm.1) | copy-start | bytes 1572868
  4.4 1.0 %copy-start.2 = (bf16[1024,256]{1,0:T(8,128)(2,1)S(1)}, bf16[1024,256]{1,0:T(8,128)(2,1)}, u32[]{:S(2)}) copy-start(bf16[1024,256]{1,0:T(8,128)(2,1)} %z_hbm.1) | copy-start | bytes 1572868
  5.5 0.8 %copy-start.3 = (f32[4,4096]{1,0:T(4,128)S(1)}, f32[4,4096]{1,0:T(4,128)}, u32[]{:S(2)}) copy-start(f32[4,4096]{1,0:T(4,128)} %bcw_ref.1) | copy-start | bytes 196612
  6.3 0.7 %copy-start.4 = (f32[4096]{0:T(1024)S(1)}, f32[4096]{0:T(1024)}, u32[]{:S(2)}) copy-start(f32[4096]{0:T(1024)} %param.20) | copy-start | bytes 49156
  7.0 0.7 %copy-start.5 = (bf16[4,1024]{1,0:T(4,128)(2,1)S(1)}, bf16[4,1024]{1,0:T(4,128)(2,1)}, u32[]{:S(2)}) copy-start(bf16[4,1024]{1,0:T(4,128)(2,1)} %dt_ref.1) | copy-start | bytes 24580
  7.7 0.7 %copy-start.6 = (f32[4,256]{1,0:T(4,128)S(1)}, f32[4,256]{1,0:T(4,128)}, u32[]{:S(2)}) copy-start(f32[4,256]{1,0:T(4,128)} %xw_ref.1) | copy-start | bytes 12292
  8.4 0.7 %copy-start.7 = (f32[256]{0:T(256)S(1)}, f32[256]{0:T(256)}, u32[]{:S(2)}) copy-start(f32[256]{0:T(256)} %param.18) | copy-start | bytes 3076
  9.1 0.7 %copy-start.8 = (f32[256]{0:T(256)S(1)}, f32[256]{0:T(256)}, u32[]{:S(2)}) copy-start(f32[256]{0:T(256)} %param.24) | copy-start | bytes 3076
  9.8 0.7 %copy-start.9 = (f32[4]{0:T(128)S(1)}, f32[4]{0:T(128)}, u32[]{:S(2)}) copy-start(f32[4]{0:T(128)} %dt_bias.1) | copy-start | bytes 52
  10.4 0.7 %copy-start.10 = (f32[4]{0:T(128)S(1)}, f32[4]{0:T(128)}, u32[]{:S(2)}) copy-start(f32[4]{0:T(128)} %a_log.1) | copy-start | bytes 52
  11.1 0.7 %copy-start.11 = (f32[4]{0:T(128)S(1)}, f32[4]{0:T(128)}, u32[]{:S(2)}) copy-start(f32[4]{0:T(128)} %skip_gain.1) | copy-start | bytes 52
  11.7 0.7 %copy-start.12 = (s32[16]{0:T(128)S(1)}, s32[16]{0:T(128)}, u32[]{:S(2)}) copy-start(s32[16]{0:T(128)} %doc_len.1) | copy-start | bytes 196

commit v2 on v1

--- a/solution.py
+++ b/solution.py
@@ -15,7 +15,7 @@
 BLOCK = 256
 TILE = 128
 HALO = 16
-CHUNKS = 4
+CHUNKS = 8
 LOG2E = math.log2(math.e)
 NORM_FLOOR = 1e-05
 F32 = jnp.float32
@@ -45,17 +45,26 @@
     x_hbm,
     bc_hbm,
     z_hbm,
+    dt_hbm,
+    xw_hbm,
+    xb_hbm,
+    bcw_hbm,
+    bcb_hbm,
+    dt_bias_hbm,
+    a_log_hbm,
+    skip_hbm,
+    nw_hbm,
+    doc_hbm,
+    out_hbm,
     dt_ref,
-    xw_ref,
-    xb_ref,
-    bcw_ref,
-    bcb_ref,
+    taps_buf,
+    bias_buf,
+    nw_ref,
     dt_bias,
     a_log,
     skip_gain,
-    nw_ref,
     doc_len,
-    out_hbm,
+    shift_buf,
     ext,
     z_buf,
     mixed,
@@ -70,6 +79,7 @@
     sums,
     out_buf,
     load_sems,
+    small_sems,
     halo_send,
     halo_recv,
     state_send,
@@ -106,6 +116,26 @@
             barrier, inc=1, device_id=(ctx, peer), device_id_type=pl.DeviceIdType.MESH
         )
 
+    pairs = [
+        (doc_hbm, doc_len),
+        (dt_hbm, dt_ref),
+        (dt_bias_hbm, dt_bias),
+        (a_log_hbm, a_log),
+        (skip_hbm, skip_gain),
+        (xw_hbm, taps_buf.at[0]),
+        (bcw_hbm.at[:, pl.ds(b_at, STATE)], taps_buf.at[1]),
+        (bcw_hbm.at[:, pl.ds(c_at, STATE)], taps_buf.at[2]),
+        (xb_hbm, bias_buf.at[0]),
+        (bcb_hbm.at[:, pl.ds(b_at, STATE)], bias_buf.at[1]),
+        (bcb_hbm.at[:, pl.ds(c_at, STATE)], bias_buf.at[2]),
+        (nw_hbm, nw_ref),
+    ]
+    smalls = [
+        pltpu.make_async_copy(src, dst, small_sems.at[i]) for i, (src, dst) in enumerate(pairs)
+    ]
+    for small in smalls:
+        small.start()
+
     own = pl.ds(HALO, rows)
     loads = [
         pltpu.make_async_copy(x_hbm, ext.at[own, pl.ds(0, width)], load_sems.at[0]),
@@ -127,31 +157,8 @@
         ext[pl.ds(0, HALO), :] = jnp.zeros((HALO, width + 2 * STATE), BF16)
         recv_buf[...] = jnp.zeros((STATE, width), BF16)
 
-    pl.semaphore_wait(barrier, n_head - 1 + jnp.where(not_last, 1, 0))
-
-    right = (jnp.minimum(ctx + 1, n_ctx - 1), me)
-    last_rows = pl.ds(rows - HALO, HALO)
-    halo_src = [
-        x_hbm.at[last_rows, :],
-        bc_hbm.at[last_rows, pl.ds(b_at, STATE)],
-        bc_hbm.at[last_rows, pl.ds(c_at, STATE)],
-    ]
-    halo_at = [pl.ds(0, width), pl.ds(width, STATE), pl.ds(width + STATE, STATE)]
-
-    def halo_copy(i):
-        return pltpu.make_async_remote_copy(
-            src_ref=halo_src[i],
-            dst_ref=ext.at[pl.ds(0, HALO), halo_at[i]],
-            send_sem=halo_send.at[i],
-            recv_sem=halo_recv.at[i],
-            device_id=right,
-            device_id_type=pl.DeviceIdType.MESH,
-        )
-
-    @pl.when(not_last)
-    def _():
-        for i in range(3):
-            halo_copy(i).start()
+    for small in smalls:
+        small.wait()
 
     first = ctx * rows
     ends, begins, total = [], [], jnp.int32(0)
@@ -216,7 +223,6 @@
     ).astype(F32)
     spread2 = jnp.concatenate([spread, spread], axis=0).astype(BF16)
     tail_buf[...] = dot(split_rows(tail_rows, 2), spread2, ((0,), (0,)))
-    entry_buf[...] = dot(split_rows(entry_rows, 2), spread2, ((0,), (0,)))
 
     decay_rows = []
     for c in range(blocks):
@@ -227,23 +233,51 @@
     for h in range(heads):
         skip_row = jnp.where(head_lane == h, skip_gain[h], skip_row)
 
+    pl.semaphore_wait(barrier, n_head - 1 + jnp.where(not_last, 1, 0))
+
+    right = (jnp.minimum(ctx + 1, n_ctx - 1), me)
+    last_rows = pl.ds(rows - HALO, HALO)
+    halo_src = [
+        x_hbm.at[last_rows, :],
+        bc_hbm.at[last_rows, pl.ds(b_at, STATE)],
+        bc_hbm.at[last_rows, pl.ds(c_at, STATE)],
+    ]
+    halo_at = [pl.ds(0, width), pl.ds(width, STATE), pl.ds(width + STATE, STATE)]
+
+    def halo_copy(i):
+        return pltpu.make_async_remote_copy(
+            src_ref=halo_src[i],
+            dst_ref=ext.at[pl.ds(0, HALO), halo_at[i]],
+            send_sem=halo_send.at[i],
+            recv_sem=halo_recv.at[i],
+            device_id=right,
+            device_id_type=pl.DeviceIdType.MESH,
+        )
+
+    @pl.when(not_last)
+    def _():
+        for i in range(3):
+            halo_copy(i).start()
+
     reach = TILE + HALO
     offset = lax.broadcasted_iota(jnp.int32, (TILE, reach), 1) - lax.broadcasted_iota(
         jnp.int32, (TILE, reach), 0
     )
     bands = [jnp.where(offset == HALO - j, 1.0, 0.0).astype(F32) for j in range(1, CONV)]
-    taps = [xw_ref[...] * 0.5] + [
-        bcw_ref[:, pl.ds(at, STATE)] * 0.5 for at in (b_at, c_at)
-    ]
-    conv_bias = [xb_ref[...] * 0.5] + [bcb_ref[:, pl.ds(at, STATE)] * 0.5 for at in (b_at, c_at)]
+    taps = [taps_buf[i] * 0.5 for i in range(3)]
+    conv_bias = [bias_buf[i] * 0.5 for i in range(3)]
     part_at = [(0, width), (width, STATE), (width + STATE, STATE)]
 
     def conv_tile(i, parts):
         at = i * TILE
-        ok = left_ext[:, at : at + reach]
-        shift = jnp.concatenate(
-            [jnp.where(ok >= j, bands[j - 1], 0.0) for j in range(1, CONV)], axis=0
-        ).astype(BF16)
+        if 0 in parts:
+            ok = left_ext[:, at : at + reach]
+            shift = jnp.concatenate(
+                [jnp.where(ok >= j, bands[j - 1], 0.0) for j in range(1, CONV)], axis=0
+            ).astype(BF16)
+            shift_buf[i] = shift
+        else:
+            shift = shift_buf[i]
         for part in parts:
             begin_at, size = part_at[part]
             source = ext[at : at + reach, begin_at : begin_at + size]
@@ -313,6 +347,7 @@
                 ).astype(BF16)
                 state_copy(i).start()
 
+    entry_buf[...] = dot(split_rows(entry_rows, 2), spread2, ((0,), (0,)))
     loads[2].wait()
     loads[3].wait()
     gap_at = lax.broadcasted_iota(jnp.int32, (BLOCK, BLOCK), 0) - lax.broadcasted_iota(
@@ -327,14 +362,16 @@
         c_c = mixed[at : at + BLOCK, width + STATE :]
         inner = dot(c_c, b_c, ((1,), (1,)))
         inner = jnp.where((gap_at >= 0) & (gap_at <= left[:, at : at + BLOCK]), inner, 0.0)
-        y = skip_row * x_c.astype(F32)
-        for h in range(heads):
-            r = c * heads + h
-            gap = jnp.minimum(run_col[:, r : r + 1] - run[r : r + 1], 0.0)
-            mix = jnp.exp2(gap) * inner * step[h : h + 1, at : at + BLOCK]
-            x_h = x_c * (head_lane == h).astype(F32).astype(BF16)
-            y = y + dot(mix.astype(BF16), x_h, ((1,), (0,)))
-        y_buf[at : at + BLOCK, :] = y
+        x_heads = [x_c * (head_lane == h).astype(F32).astype(BF16) for h in range(heads)]
+        for lo in range(0, BLOCK, TILE):
+            hi = lo + TILE
+            y = skip_row * x_c[lo:hi].astype(F32)
+            for h in range(heads):
+                r = c * heads + h
+                gap = jnp.minimum(run_col[lo:hi, r : r + 1] - run[r : r + 1, :hi], 0.0)
+                mix = jnp.exp2(gap) * inner[lo:hi, :hi] * step[h : h + 1, at : at + hi]
+                y = y + dot(mix.astype(BF16), x_heads[h][:hi], ((1,), (0,)))
+            y_buf[at + lo : at + hi, :] = y
         gate_buf[at : at + BLOCK, :] = silu_half(z_buf[at : at + BLOCK, :].astype(F32) * 0.5)
         forward(c + 1)
 
@@ -432,15 +469,24 @@
     blocks = rows // BLOCK
     tiles = rows // TILE
     anywhere = pl.BlockSpec(memory_space=pltpu.HBM)
-    vmem = pl.BlockSpec(memory_space=pltpu.VMEM)
-    smem = pl.BlockSpec(memory_space=pltpu.SMEM)
+    heads = dt_in.shape[0]
+    docs = doc_len.shape[0]
     dma = pltpu.SemaphoreType.DMA
     return pl.pallas_call(
         functools.partial(layer_kernel, n_ctx, n_head),
         out_shape=jax.ShapeDtypeStruct((rows, width), BF16),
-        in_specs=[anywhere] * 3 + [vmem] * 5 + [smem] * 3 + [vmem, smem],
+        in_specs=[anywhere] * 13,
         out_specs=anywhere,
         scratch_shapes=[
+            pltpu.VMEM((heads, rows), BF16),
+            pltpu.VMEM((3, CONV, width), F32),
+            pltpu.VMEM((3, 1, width), F32),
+            pltpu.VMEM((1, width), F32),
+            pltpu.SMEM((heads,), F32),
+            pltpu.SMEM((heads,), F32),
+            pltpu.SMEM((heads,), F32),
+            pltpu.SMEM((docs,), jnp.int32),
+            pltpu.VMEM((tiles, (CONV - 1) * TILE, TILE + HALO), BF16),
             pltpu.VMEM((rows + HALO, width + 2 * STATE), BF16),
             pltpu.VMEM((rows, width), BF16),
             pltpu.VMEM((rows, width + 2 * STATE), BF16),
@@ -455,6 +501,7 @@
             pltpu.VMEM((n_head, tiles, TILE), F32),
             pltpu.VMEM((rows, width), BF16),
             dma((4,)),
+            dma((12,)),
             dma((3,)),
             dma((3,)),
             dma((CHUNKS,)),
@@ -464,7 +511,7 @@
             dma((blocks,)),
         ],
         compiler_params=pltpu.CompilerParams(
-            collective_id=0, has_side_effects=True, vmem_limit_bytes=40 * 1024 * 1024
+            collective_id=0, has_side_effects=True, vmem_limit_bytes=60 * 1024 * 1024
         ),
     )(
         x_in,

time: 33.4 us -> 20.4 us (0.61); the launches traced: 32.9 us -> 20.2 us
  local copies, waits for them, and re-layouts: 13.2 us -> 1.87 us
  Pallas kernels: 19.7 us -> 18.4 us
    unnamed x27 -> x1, local copies, waits for them, and re-layouts: 13.2 us -> 1.87 us
    pallas_call x1, Pallas kernels: 19.7 us -> 18.4 us  [shards(): pl.pallas_call(functools.partial(layer_kernel, n_ctx, n_head), out_shape=...]
where the time goes in v2:
time: 20.4 us; the launch traced here: 20.2 us
  Pallas kernels  18.4 us (90%)
  local copies, waits for them, and re-layouts  1.87 us (9%)
    pallas_call x1, Pallas kernels, shards(): pl.pallas_call(functools.partial(layer_kernel, n_ctx, n_head), out_shape=...  18.4 us
    unnamed x1, local copies, waits for them, and re-layouts  1.87 us

profile of v2, /device:TPU:25, one launch (start us, length us, event | category | flops | bytes accessed | tf_op | source)
XLA Modules:
  0.0 20.2 jit_solution(1375284133899308201)
XLA Ops:
  0.0 18.4 %shard_map.127 = bf16[1024,256]{1,0:T(8,128)(2,1)} custom-call(bf16[1024,256]{1,0:T(8,128)(2,1)} %x_hbm.1, bf16[1024,4096]{1,0:T(8,128)(2,1)} %bc_hbm.1, bf16[1024,256]{1,0:T(8,128)(2,1)} %z_hbm.1, bf16[4,1024]{1,0:T(4,128)(2,1)} %dt_hbm.1, f32[4,256]{1,0:T(4,128)} %xw_hbm.1, f32[1,256]{1,0:T(1,128)} %bitcast.4, f32[4,4096]{1,0:T(4,128)} %bcw_hbm.1, ...), custom_call_target="tpu_custom_call" | custom-call | tf_op jit(solution)/shard_map/pallas_call | solution.py:475
  18.4 1.9 %copy.15 = bf16[1024,256]{1,0:T(8,128)(2,1)} copy(bf16[1024,256]{1,0:T(8,128)(2,1)} %shard_map.127) | data formatting | bytes 1048576

commit v3 on v2

--- a/solution.py
+++ b/solution.py
@@ -55,7 +55,8 @@
     skip_hbm,
     nw_hbm,
     doc_hbm,
-    out_hbm,
+    gated_ref,
+    scale_ref,
     dt_ref,
     taps_buf,
     bias_buf,
@@ -77,7 +78,6 @@
     send_buf,
     recv_buf,
     sums,
-    out_buf,
     load_sems,
     small_sems,
     halo_send,
@@ -86,7 +86,6 @@
     state_recv,
     sums_send,
     sums_recv,
-    out_sems,
 ):
     rows = x_hbm.shape[0]
     width = x_hbm.shape[1]
@@ -334,12 +333,16 @@
             send_buf[at, :] = end_buf[at, :].astype(BF16)
             state_copy(i).start()
 
+    half = CHUNKS // 2
+
     def forward(stage):
-        mine = ctx == stage if stage < blocks else ctx >= stage
+        early = stage <= 2
+        mine = (ctx == 1) if early else (ctx >= 2)
+        begin_at = half * ((stage - 1) % 2)
 
         @pl.when(mine & not_last)
         def _():
-            for i in range(CHUNKS):
+            for i in range(begin_at, begin_at + half):
                 at = pl.ds(i * chunk, chunk)
                 state_copy(i).wait_recv()
                 send_buf[at, :] = (
@@ -380,6 +383,7 @@
         for i in range(CHUNKS):
             state_copy(i).wait_recv()
 
+    norm_row = nw_ref[...]
     entering = recv_buf[...].astype(F32)
     so_far = jnp.ones((1, width), F32)
     ones = jnp.ones((8, width), BF16)
@@ -392,7 +396,7 @@
         from_state = dot(mixed[at : at + BLOCK, width + STATE :], incoming, ((1,), (0,)))
         y = y_buf[at : at + BLOCK, :] + entry_buf[at : at + BLOCK, :] * from_state
         gated = y * gate_buf[at : at + BLOCK, :]
-        y_buf[at : at + BLOCK, :] = gated
+        gated_ref[at : at + BLOCK, :] = gated * norm_row
         row = dot(ones, (gated * gated).astype(BF16), ((1,), (1,)))
         for i in range(BLOCK // TILE):
             squares = jnp.where(
@@ -417,22 +421,7 @@
     every = sums[0]
     for d in range(1, n_head):
         every = every + sums[d]
-    scale = lax.rsqrt(every / (n_head * width) + NORM_FLOOR)
-    norm_row = nw_ref[...]
-    stores = []
-    for c in range(blocks):
-        at = c * BLOCK
-        for i in range(BLOCK // TILE):
-            t = c * (BLOCK // TILE) + i
-            column = jnp.transpose(jnp.broadcast_to(scale[t : t + 1, :], (TILE, TILE)))
-            column = jnp.concatenate([column] * (width // TILE), axis=1)
-            piece = y_buf[t * TILE : (t + 1) * TILE, :] * column * norm_row
-            out_buf[t * TILE : (t + 1) * TILE, :] = piece.astype(BF16)
-        store = pltpu.make_async_copy(
-            out_buf.at[pl.ds(at, BLOCK), :], out_hbm.at[pl.ds(at, BLOCK), :], out_sems.at[c]
-        )
-        store.start()
-        stores.append(store)
+    scale_ref[...] = lax.rsqrt(every / (n_head * width) + NORM_FLOOR)
 
     for d in range(n_head - 1):
         sums_copy(d).wait_send()
@@ -444,6 +433,22 @@
         for i in range(CHUNKS):
             state_copy(i).wait_send()
 
+
+def scale_kernel(gated_ref, scale_ref, out_hbm, out_buf, out_sems):
+    rows, width = gated_ref.shape
+    stores = []
+    for t in range(rows // TILE):
+        at = pl.ds(t * TILE, TILE)
+        column = jnp.transpose(jnp.broadcast_to(scale_ref[t : t + 1, :], (TILE, TILE)))
+        column = jnp.concatenate([column] * (width // TILE), axis=1)
+        out_buf[at, :] = (gated_ref[at, :] * column).astype(BF16)
+        if t % 2 == 1:
+            pair = pl.ds((t - 1) * TILE, 2 * TILE)
+            store = pltpu.make_async_copy(
+                out_buf.at[pair, :], out_hbm.at[pair, :], out_sems.at[t // 2]
+            )
+            store.start()
+            stores.append(store)
     for store in stores:
         store.wait()
 
@@ -471,12 +476,13 @@
     anywhere = pl.BlockSpec(memory_space=pltpu.HBM)
     heads = dt_in.shape[0]
     docs = doc_len.shape[0]
+    vmem = pl.BlockSpec(memory_space=pltpu.VMEM)
     dma = pltpu.SemaphoreType.DMA
-    return pl.pallas_call(
+    gated, scale = pl.pallas_call(
         functools.partial(layer_kernel, n_ctx, n_head),
-        out_shape=jax.ShapeDtypeStruct((rows, width), BF16),
+        out_shape=(pltpu.VMEM((rows, width), F32), pltpu.VMEM((tiles, TILE), F32)),
         in_specs=[anywhere] * 13,
-        out_specs=anywhere,
+        out_specs=(vmem, vmem),
         scratch_shapes=[
             pltpu.VMEM((heads, rows), BF16),
             pltpu.VMEM((3, CONV, width), F32),
@@ -499,7 +505,6 @@
             pltpu.VMEM((STATE, width), BF16),
             pltpu.VMEM((STATE, width), BF16),
             pltpu.VMEM((n_head, tiles, TILE), F32),
-            pltpu.VMEM((rows, width), BF16),
             dma((4,)),
             dma((12,)),
             dma((3,)),
@@ -508,7 +513,6 @@
             dma((CHUNKS,)),
             dma((n_head - 1,)),
             dma((n_head - 1,)),
-            dma((blocks,)),
         ],
         compiler_params=pltpu.CompilerParams(
             collective_id=0, has_side_effects=True, vmem_limit_bytes=60 * 1024 * 1024
@@ -528,6 +532,14 @@
         norm_w.reshape(1, -1),
         doc_len,
     )
+    return pl.pallas_call(
+        scale_kernel,
+        out_shape=jax.ShapeDtypeStruct((rows, width), BF16),
+        in_specs=[vmem, vmem],
+        out_specs=anywhere,
+        scratch_shapes=[pltpu.VMEM((rows, width), BF16), dma((tiles // 2,))],
+        compiler_params=pltpu.CompilerParams(vmem_limit_bytes=4 * 1024 * 1024),
+    )(gated, scale)
 
 
 def solution(mesh):

time: 20.4 us -> 19.1 us (0.936)
  local copies, waits for them, and re-layouts: 1.87 us -> 0 us
  Pallas kernels: 18.4 us -> 18.9 us
    unnamed x1 -> x0, local copies, waits for them, and re-layouts: 1.87 us -> none
    pallas_call x0 -> x1, Pallas kernels: none -> 0.92 us  [shards(): pl.pallas_call(scale_kernel, out_shape=jax.ShapeDtypeStruct((rows, width)...]
    pallas_call x1, Pallas kernels: 18.4 us -> 18 us  [shards(): pl.pallas_call(functools.partial(layer_kernel, n_ctx, n_head), out_shape=...]
where the time goes in v3:
time: 19.1 us; the launch traced here: 18.9 us
  Pallas kernels  18.9 us (99%)
    pallas_call x1, Pallas kernels, shards(): pl.pallas_call(functools.partial(layer_kernel, n_ctx, n_head), out_shape=...  18 us
    pallas_call x1, Pallas kernels, shards(): pl.pallas_call(scale_kernel, out_shape=jax.ShapeDtypeStruct((rows, width)...  0.92 us

profile of v3, /device:TPU:25, one launch (start us, length us, event | category | flops | bytes accessed | tf_op | source)
XLA Modules:
  0.0 18.9 jit_solution(9834904965339369618)
XLA Ops:
  0.0 18.0 %shard_map.127 = (f32[1024,256]{1,0:T(8,128)S(1)}, f32[8,128]{1,0:T(8,128)S(1)}) custom-call(bf16[1024,256]{1,0:T(8,128)(2,1)} %x_hbm.1, bf16[1024,4096]{1,0:T(8,128)(2,1)} %bc_hbm.1, bf16[1024,256]{1,0:T(8,128)(2,1)} %z_hbm.1, bf16[4,1024]{1,0:T(4,128)(2,1)} %dt_hbm.1, f32[4,256]{1,0:T(4,128)} %xw_hbm.1, f32[1,256]{1,0:T(1,128)} %bitcast.4, ...), custom_call_target="tpu_custom_call" | custom-call | tf_op jit(solution)/shard_map/pallas_call | solution.py:481
  18.0 0.9 %shard_map.128 = bf16[1024,256]{1,0:T(8,128)(2,1)} custom-call(f32[1024,256]{1,0:T(8,128)S(1)} %get-tuple-element.7.gated_ref, f32[8,128]{1,0:T(8,128)S(1)} %get-tuple-element.8.scale_ref), custom_call_target="tpu_custom_call" | custom-call | tf_op jit(solution)/shard_map/pallas_call | solution.py:535

commit v4 on v3

--- a/solution.py
+++ b/solution.py
@@ -15,7 +15,7 @@
 BLOCK = 256
 TILE = 128
 HALO = 16
-CHUNKS = 8
+CHUNKS = 4
 LOG2E = math.log2(math.e)
 NORM_FLOOR = 1e-05
 F32 = jnp.float32
@@ -100,6 +100,7 @@
     b_at = pl.multiple_of(group * STATE, STATE)
     c_at = pl.multiple_of((GROUPS + group) * STATE, STATE)
     not_last = ctx < n_ctx - 1
+    rounds = recv_buf.shape[0]
 
     barrier = pltpu.get_barrier_semaphore()
 
@@ -154,7 +155,7 @@
     @pl.when(ctx == 0)
     def _():
         ext[pl.ds(0, HALO), :] = jnp.zeros((HALO, width + 2 * STATE), BF16)
-        recv_buf[...] = jnp.zeros((STATE, width), BF16)
+        recv_buf[...] = jnp.zeros(recv_buf.shape, BF16)
 
     for small in smalls:
         small.wait()
@@ -315,40 +316,43 @@
 
     chunk = STATE // CHUNKS
 
-    def state_copy(i):
+    def state_copy(turn, i):
         at = pl.ds(i * chunk, chunk)
         return pltpu.make_async_remote_copy(
-            src_ref=send_buf.at[at, :],
-            dst_ref=recv_buf.at[at, :],
-            send_sem=state_send.at[i],
-            recv_sem=state_recv.at[i],
+            src_ref=send_buf.at[turn, at, :],
+            dst_ref=recv_buf.at[turn, at, :],
+            send_sem=state_send.at[turn, i],
+            recv_sem=state_recv.at[turn, i],
             device_id=right,
             device_id_type=pl.DeviceIdType.MESH,
         )
 
-    @pl.when(ctx == 0)
+    @pl.when(not_last)
     def _():
         for i in range(CHUNKS):
             at = pl.ds(i * chunk, chunk)
-            send_buf[at, :] = end_buf[at, :].astype(BF16)
-            state_copy(i).start()
-
-    half = CHUNKS // 2
-
-    def forward(stage):
-        early = stage <= 2
-        mine = (ctx == 1) if early else (ctx >= 2)
-        begin_at = half * ((stage - 1) % 2)
-
-        @pl.when(mine & not_last)
+            send_buf[0, at, :] = end_buf[at, :].astype(BF16)
+            state_copy(0, i).start()
+
+    def arrived(turn, chunks):
+        @pl.when(ctx > 0)
         def _():
-            for i in range(begin_at, begin_at + half):
+            for i in chunks:
+                state_copy(turn, i).wait_recv()
+
+    def pass_on(turn, chunks):
+        for i in chunks:
+            arrived(turn, [i])
+
+            @pl.when(not_last)
+            def _():
                 at = pl.ds(i * chunk, chunk)
-                state_copy(i).wait_recv()
-                send_buf[at, :] = (
-                    end_buf[at, :] + shard_decay * recv_buf[at, :].astype(F32)
+                send_buf[turn + 1, at, :] = (
+                    end_buf[at, :] + shard_decay * recv_buf[turn, at, :].astype(F32)
                 ).astype(BF16)
-                state_copy(i).start()
+                state_copy(turn + 1, i).start()
+
+    halves = [range(0, CHUNKS // 2), range(CHUNKS // 2, CHUNKS)]
 
     entry_buf[...] = dot(split_rows(entry_rows, 2), spread2, ((0,), (0,)))
     loads[2].wait()
@@ -375,26 +379,33 @@
                 mix = jnp.exp2(gap) * inner[lo:hi, :hi] * step[h : h + 1, at : at + hi]
                 y = y + dot(mix.astype(BF16), x_heads[h][:hi], ((1,), (0,)))
             y_buf[at + lo : at + hi, :] = y
+        if rounds > 1 and c >= blocks - 2:
+            pass_on(0, halves[c - (blocks - 2)])
+
+    for turn in range(1, rounds - 1):
+        pass_on(turn, range(CHUNKS))
+    for c in range(blocks):
+        at = c * BLOCK
         gate_buf[at : at + BLOCK, :] = silu_half(z_buf[at : at + BLOCK, :].astype(F32) * 0.5)
-        forward(c + 1)
-
-    @pl.when(ctx == n_ctx - 1)
-    def _():
-        for i in range(CHUNKS):
-            state_copy(i).wait_recv()
+        if c > 0:
+            local = dot(
+                mixed[at : at + BLOCK, width + STATE :], state_buf[c].astype(BF16), ((1,), (0,))
+            )
+            y_buf[at : at + BLOCK, :] += entry_buf[at : at + BLOCK, :] * local
+
+    arrived(rounds - 1, range(CHUNKS))
 
     norm_row = nw_ref[...]
-    entering = recv_buf[...].astype(F32)
+    entering = recv_buf[rounds - 1]
     so_far = jnp.ones((1, width), F32)
     ones = jnp.ones((8, width), BF16)
     slot_row = lax.broadcasted_iota(jnp.int32, (tiles, TILE), 0)
     squares = jnp.zeros((tiles, TILE), F32)
     for c in range(blocks):
         at = c * BLOCK
-        incoming = (state_buf[c] + so_far * entering).astype(BF16)
+        from_state = dot(mixed[at : at + BLOCK, width + STATE :], entering, ((1,), (0,)))
+        y = y_buf[at : at + BLOCK, :] + entry_buf[at : at + BLOCK, :] * so_far * from_state
         so_far = so_far * decay_rows[c]
-        from_state = dot(mixed[at : at + BLOCK, width + STATE :], incoming, ((1,), (0,)))
-        y = y_buf[at : at + BLOCK, :] + entry_buf[at : at + BLOCK, :] * from_state
         gated = y * gate_buf[at : at + BLOCK, :]
         gated_ref[at : at + BLOCK, :] = gated * norm_row
         row = dot(ones, (gated * gated).astype(BF16), ((1,), (1,)))
@@ -430,8 +441,9 @@
     def _():
         for i in range(3):
             halo_copy(i).wait_send()
-        for i in range(CHUNKS):
-            state_copy(i).wait_send()
+        for turn in range(rounds):
+            for i in range(CHUNKS):
+                state_copy(turn, i).wait_send()
 
 
 def scale_kernel(gated_ref, scale_ref, out_hbm, out_buf, out_sems):
@@ -471,6 +483,7 @@
     rows, width = x_in.shape
     n_ctx = lax.axis_size("context")
     n_head = lax.axis_size("head")
+    rounds = max(1, n_ctx // 2)
     blocks = rows // BLOCK
     tiles = rows // TILE
     anywhere = pl.BlockSpec(memory_space=pltpu.HBM)
@@ -502,15 +515,15 @@
             pltpu.VMEM((STATE, width), F32),
             pltpu.VMEM((rows, width), F32),
             pltpu.VMEM((rows, width), F32),
-            pltpu.VMEM((STATE, width), BF16),
-            pltpu.VMEM((STATE, width), BF16),
+            pltpu.VMEM((rounds, STATE, width), BF16),
+            pltpu.VMEM((rounds, STATE, width), BF16),
             pltpu.VMEM((n_head, tiles, TILE), F32),
             dma((4,)),
             dma((12,)),
             dma((3,)),
             dma((3,)),
-            dma((CHUNKS,)),
-            dma((CHUNKS,)),
+            dma((rounds, CHUNKS)),
+            dma((rounds, CHUNKS)),
             dma((n_head - 1,)),
             dma((n_head - 1,)),
         ],

time: 19.1 us -> 18.7 us (0.979)
  Pallas kernels: 18.9 us -> 18.6 us
    pallas_call x1, Pallas kernels: 18 us -> 17.6 us  [shards(): pl.pallas_call(functools.partial(layer_kernel, n_ctx, n_head), out_shape=...]
where the time goes in v4:
time: 18.7 us; the launch traced here: 18.6 us
  Pallas kernels  18.6 us (99%)
    pallas_call x1, Pallas kernels, shards(): pl.pallas_call(functools.partial(layer_kernel, n_ctx, n_head), out_shape=...  17.6 us
    pallas_call x1, Pallas kernels, shards(): pl.pallas_call(scale_kernel, out_shape=jax.ShapeDtypeStruct((rows, width)...  0.92 us

profile of v4, /device:TPU:25, one launch (start us, length us, event | category | flops | bytes accessed | tf_op | source)
XLA Modules:
  0.0 18.6 jit_solution(13063952964110039783)
XLA Ops:
  0.0 17.6 %shard_map.127 = (f32[1024,256]{1,0:T(8,128)S(1)}, f32[8,128]{1,0:T(8,128)S(1)}) custom-call(bf16[1024,256]{1,0:T(8,128)(2,1)} %x_hbm.1, bf16[1024,4096]{1,0:T(8,128)(2,1)} %bc_hbm.1, bf16[1024,256]{1,0:T(8,128)(2,1)} %z_hbm.1, bf16[4,1024]{1,0:T(4,128)(2,1)} %dt_hbm.1, f32[4,256]{1,0:T(4,128)} %xw_hbm.1, f32[1,256]{1,0:T(1,128)} %bitcast.4, ...), custom_call_target="tpu_custom_call" | custom-call | tf_op jit(solution)/shard_map/pallas_call | solution.py:494
  17.7 0.9 %shard_map.128 = bf16[1024,256]{1,0:T(8,128)(2,1)} custom-call(f32[1024,256]{1,0:T(8,128)S(1)} %get-tuple-element.7.gated_ref, f32[8,128]{1,0:T(8,128)S(1)} %get-tuple-element.8.scale_ref), custom_call_target="tpu_custom_call" | custom-call | tf_op jit(solution)/shard_map/pallas_call | solution.py:548

commit v5 on v3

--- a/solution.py
+++ b/solution.py
@@ -77,6 +77,7 @@
     gate_buf,
     send_buf,
     recv_buf,
+    x_tail_buf,
     sums,
     load_sems,
     small_sems,
@@ -263,9 +264,17 @@
         jnp.int32, (TILE, reach), 0
     )
     bands = [jnp.where(offset == HALO - j, 1.0, 0.0).astype(F32) for j in range(1, CONV)]
-    taps = [taps_buf[i] * 0.5 for i in range(3)]
-    conv_bias = [bias_buf[i] * 0.5 for i in range(3)]
-    part_at = [(0, width), (width, STATE), (width + STATE, STATE)]
+    taps_in = [taps_buf[i] * 0.5 for i in range(3)]
+    bias_in = [bias_buf[i] * 0.5 for i in range(3)]
+    part_half = STATE // 2
+    taps = [taps_in[0], taps_in[1][:, :part_half], taps_in[1][:, part_half:], taps_in[2]]
+    conv_bias = [bias_in[0], bias_in[1][:, :part_half], bias_in[1][:, part_half:], bias_in[2]]
+    part_at = [
+        (0, width),
+        (width, part_half),
+        (width + part_half, part_half),
+        (width + STATE, STATE),
+    ]
 
     def conv_tile(i, parts):
         at = i * TILE
@@ -299,20 +308,9 @@
 
     conv_tile(0, (0, 1))
 
-    state = jnp.zeros((STATE, width), F32)
-    for c in range(blocks):
-        at = c * BLOCK
-        state_buf[c] = state
-        x_tail = (mixed[at : at + BLOCK, :width].astype(F32) * tail_buf[at : at + BLOCK, :]).astype(
-            BF16
-        )
-        summary = dot(mixed[at : at + BLOCK, width : width + STATE], x_tail, ((0,), (0,)))
-        state = state * decay_rows[c] + summary
-    end_buf[...] = state
     shard_decay = decay_rows[0]
     for c in range(1, blocks):
         shard_decay = shard_decay * decay_rows[c]
-
     chunk = STATE // CHUNKS
 
     def state_copy(i):
@@ -326,23 +324,38 @@
             device_id_type=pl.DeviceIdType.MESH,
         )
 
-    @pl.when(ctx == 0)
-    def _():
-        for i in range(CHUNKS):
-            at = pl.ds(i * chunk, chunk)
-            send_buf[at, :] = end_buf[at, :].astype(BF16)
-            state_copy(i).start()
-
-    half = CHUNKS // 2
-
-    def forward(stage):
-        early = stage <= 2
-        mine = (ctx == 1) if early else (ctx >= 2)
-        begin_at = half * ((stage - 1) % 2)
-
-        @pl.when(mine & not_last)
+    def half_states(half):
+        columns = slice(half * part_half, (half + 1) * part_half)
+        state = jnp.zeros((part_half, width), F32)
+        for c in range(blocks):
+            block = slice(c * BLOCK, (c + 1) * BLOCK)
+            state_buf[c, columns, :] = state
+            if half == 0:
+                x_tail_buf[block, :] = (
+                    mixed[block, :width].astype(F32) * tail_buf[block, :]
+                ).astype(BF16)
+            b_half = mixed[block, width + columns.start : width + columns.stop]
+            state = state * decay_rows[c] + dot(b_half, x_tail_buf[block, :], ((0,), (0,)))
+        end_buf[columns, :] = state
+
+        @pl.when((ctx == 0) & not_last)
         def _():
-            for i in range(begin_at, begin_at + half):
+            send_buf[columns, :] = end_buf[columns, :].astype(BF16)
+            for i in range(half * CHUNKS // 2, (half + 1) * CHUNKS // 2):
+                state_copy(i).start()
+
+    half_states(0)
+    for i in range(tiles):
+        conv_tile(i, (2,))
+    half_states(1)
+
+    def pass_on(turn, chunks):
+        if not chunks:
+            return
+
+        @pl.when(turn & not_last)
+        def _():
+            for i in chunks:
                 at = pl.ds(i * chunk, chunk)
                 state_copy(i).wait_recv()
                 send_buf[at, :] = (
@@ -359,7 +372,7 @@
     for c in range(blocks):
         at = c * BLOCK
         for i in range(BLOCK // TILE):
-            conv_tile(c * (BLOCK // TILE) + i, (2,))
+            conv_tile(c * (BLOCK // TILE) + i, (3,))
         x_c = mixed[at : at + BLOCK, :width]
         b_c = mixed[at : at + BLOCK, width : width + STATE]
         c_c = mixed[at : at + BLOCK, width + STATE :]
@@ -375,26 +388,38 @@
                 mix = jnp.exp2(gap) * inner[lo:hi, :hi] * step[h : h + 1, at : at + hi]
                 y = y + dot(mix.astype(BF16), x_heads[h][:hi], ((1,), (0,)))
             y_buf[at + lo : at + hi, :] = y
+            done = c * (BLOCK // TILE) + lo // TILE
+            pass_on(ctx == 1, [done] if done < CHUNKS else [])
+            pass_on(ctx == 2, [done - 2] if 2 <= done < CHUNKS + 2 else [])
+
+    pass_on(ctx == 1, list(range(tiles, CHUNKS)))
+    pass_on(ctx == 2, list(range(tiles - 2, CHUNKS)))
+    pass_on(ctx >= 3, list(range(CHUNKS)))
+    for c in range(blocks):
+        at = c * BLOCK
         gate_buf[at : at + BLOCK, :] = silu_half(z_buf[at : at + BLOCK, :].astype(F32) * 0.5)
-        forward(c + 1)
-
-    @pl.when(ctx == n_ctx - 1)
+        if c > 0:
+            local = dot(
+                mixed[at : at + BLOCK, width + STATE :], state_buf[c].astype(BF16), ((1,), (0,))
+            )
+            y_buf[at : at + BLOCK, :] += entry_buf[at : at + BLOCK, :] * local
+
+    @pl.when((ctx > 0) & (ctx == n_ctx - 1))
     def _():
         for i in range(CHUNKS):
             state_copy(i).wait_recv()
 
     norm_row = nw_ref[...]
-    entering = recv_buf[...].astype(F32)
+    entering = recv_buf[...]
     so_far = jnp.ones((1, width), F32)
     ones = jnp.ones((8, width), BF16)
     slot_row = lax.broadcasted_iota(jnp.int32, (tiles, TILE), 0)
     squares = jnp.zeros((tiles, TILE), F32)
     for c in range(blocks):
         at = c * BLOCK
-        incoming = (state_buf[c] + so_far * entering).astype(BF16)
+        from_state = dot(mixed[at : at + BLOCK, width + STATE :], entering, ((1,), (0,)))
+        y = y_buf[at : at + BLOCK, :] + entry_buf[at : at + BLOCK, :] * so_far * from_state
         so_far = so_far * decay_rows[c]
-        from_state = dot(mixed[at : at + BLOCK, width + STATE :], incoming, ((1,), (0,)))
-        y = y_buf[at : at + BLOCK, :] + entry_buf[at : at + BLOCK, :] * from_state
         gated = y * gate_buf[at : at + BLOCK, :]
         gated_ref[at : at + BLOCK, :] = gated * norm_row
         row = dot(ones, (gated * gated).astype(BF16), ((1,), (1,)))
@@ -504,6 +529,7 @@
             pltpu.VMEM((rows, width), F32),
             pltpu.VMEM((STATE, width), BF16),
             pltpu.VMEM((STATE, width), BF16),
+            pltpu.VMEM((rows, width), BF16),
             pltpu.VMEM((n_head, tiles, TILE), F32),
             dma((4,)),
             dma((12,)),

time: 19.1 us -> 21.2 us (1.11)
  Pallas kernels: 18.9 us -> 21.1 us
    pallas_call x1, Pallas kernels: 18 us -> 20.2 us  [shards(): pl.pallas_call(functools.partial(layer_kernel, n_ctx, n_head), out_shape=...]
where the time goes in v5:
time: 21.2 us; the launch traced here: 21.1 us
  Pallas kernels  21.1 us (100%)
    pallas_call x1, Pallas kernels, shards(): pl.pallas_call(functools.partial(layer_kernel, n_ctx, n_head), out_shape=...  20.2 us
    pallas_call x1, Pallas kernels, shards(): pl.pallas_call(scale_kernel, out_shape=jax.ShapeDtypeStruct((rows, width)...  0.92 us

profile of v5, /device:TPU:25, one launch (start us, length us, event | category | flops | bytes accessed | tf_op | source)
XLA Modules:
  0.0 21.1 jit_solution(15173527317888487234)
XLA Ops:
  0.0 20.2 %shard_map.127 = (f32[1024,256]{1,0:T(8,128)S(1)}, f32[8,128]{1,0:T(8,128)S(1)}) custom-call(bf16[1024,256]{1,0:T(8,128)(2,1)} %x_hbm.1, bf16[1024,4096]{1,0:T(8,128)(2,1)} %bc_hbm.1, bf16[1024,256]{1,0:T(8,128)(2,1)} %z_hbm.1, bf16[4,1024]{1,0:T(4,128)(2,1)} %dt_hbm.1, f32[4,256]{1,0:T(4,128)} %xw_hbm.1, f32[1,256]{1,0:T(1,128)} %bitcast.4, ...), custom_call_target="tpu_custom_call" | custom-call | tf_op jit(solution)/shard_map/pallas_call | solution.py:506
  20.2 0.9 %shard_map.128 = bf16[1024,256]{1,0:T(8,128)(2,1)} custom-call(f32[1024,256]{1,0:T(8,128)S(1)} %get-tuple-element.7.gated_ref, f32[8,128]{1,0:T(8,128)S(1)} %get-tuple-element.8.scale_ref), custom_call_target="tpu_custom_call" | custom-call | tf_op jit(solution)/shard_map/pallas_call | solution.py:561

commit v6 on v3

--- a/solution.py
+++ b/solution.py
@@ -326,29 +326,25 @@
             device_id_type=pl.DeviceIdType.MESH,
         )
 
-    @pl.when(ctx == 0)
+    @pl.when((ctx == 0) & not_last)
     def _():
         for i in range(CHUNKS):
             at = pl.ds(i * chunk, chunk)
             send_buf[at, :] = end_buf[at, :].astype(BF16)
             state_copy(i).start()
 
-    half = CHUNKS // 2
-
-    def forward(stage):
-        early = stage <= 2
-        mine = (ctx == 1) if early else (ctx >= 2)
-        begin_at = half * ((stage - 1) % 2)
-
-        @pl.when(mine & not_last)
+    def pass_on(turn, chunks):
+        @pl.when(turn & not_last)
         def _():
-            for i in range(begin_at, begin_at + half):
+            for i in chunks:
                 at = pl.ds(i * chunk, chunk)
                 state_copy(i).wait_recv()
                 send_buf[at, :] = (
                     end_buf[at, :] + shard_decay * recv_buf[at, :].astype(F32)
                 ).astype(BF16)
                 state_copy(i).start()
+
+    pace = CHUNKS // blocks
 
     entry_buf[...] = dot(split_rows(entry_rows, 2), spread2, ((0,), (0,)))
     loads[2].wait()
@@ -375,26 +371,37 @@
                 mix = jnp.exp2(gap) * inner[lo:hi, :hi] * step[h : h + 1, at : at + hi]
                 y = y + dot(mix.astype(BF16), x_heads[h][:hi], ((1,), (0,)))
             y_buf[at + lo : at + hi, :] = y
+        pass_on(ctx == 1, range(c * pace, (c + 1) * pace))
+        if c >= 2:
+            pass_on(ctx == 2, range((c - 2) * pace, (c - 1) * pace))
+
+    pass_on(ctx == 2, range(max(0, blocks - 2) * pace, CHUNKS))
+    pass_on(ctx >= 3, range(CHUNKS))
+    for c in range(blocks):
+        at = c * BLOCK
         gate_buf[at : at + BLOCK, :] = silu_half(z_buf[at : at + BLOCK, :].astype(F32) * 0.5)
-        forward(c + 1)
-
-    @pl.when(ctx == n_ctx - 1)
+        if c > 0:
+            local = dot(
+                mixed[at : at + BLOCK, width + STATE :], state_buf[c].astype(BF16), ((1,), (0,))
+            )
+            y_buf[at : at + BLOCK, :] += entry_buf[at : at + BLOCK, :] * local
+
+    @pl.when((ctx > 0) & (ctx == n_ctx - 1))
     def _():
         for i in range(CHUNKS):
             state_copy(i).wait_recv()
 
     norm_row = nw_ref[...]
-    entering = recv_buf[...].astype(F32)
+    entering = recv_buf[...]
     so_far = jnp.ones((1, width), F32)
     ones = jnp.ones((8, width), BF16)
     slot_row = lax.broadcasted_iota(jnp.int32, (tiles, TILE), 0)
     squares = jnp.zeros((tiles, TILE), F32)
     for c in range(blocks):
         at = c * BLOCK
-        incoming = (state_buf[c] + so_far * entering).astype(BF16)
+        from_state = dot(mixed[at : at + BLOCK, width + STATE :], entering, ((1,), (0,)))
+        y = y_buf[at : at + BLOCK, :] + entry_buf[at : at + BLOCK, :] * so_far * from_state
         so_far = so_far * decay_rows[c]
-        from_state = dot(mixed[at : at + BLOCK, width + STATE :], incoming, ((1,), (0,)))
-        y = y_buf[at : at + BLOCK, :] + entry_buf[at : at + BLOCK, :] * from_state
         gated = y * gate_buf[at : at + BLOCK, :]
         gated_ref[at : at + BLOCK, :] = gated * norm_row
         row = dot(ones, (gated * gated).astype(BF16), ((1,), (1,)))

time: 19.1 us -> 19.9 us (1.042)
  Pallas kernels: 18.9 us -> 19.7 us
    pallas_call x1, Pallas kernels: 18 us -> 18.8 us  [shards(): pl.pallas_call(functools.partial(layer_kernel, n_ctx, n_head), out_shape=...]
where the time goes in v6:
time: 19.9 us; the launch traced here: 19.7 us
  Pallas kernels  19.7 us (99%)
    pallas_call x1, Pallas kernels, shards(): pl.pallas_call(functools.partial(layer_kernel, n_ctx, n_head), out_shape=...  18.8 us
    pallas_call x1, Pallas kernels, shards(): pl.pallas_call(scale_kernel, out_shape=jax.ShapeDtypeStruct((rows, width)...  0.92 us

profile of v6, /device:TPU:25, one launch (start us, length us, event | category | flops | bytes accessed | tf_op | source)
XLA Modules:
  0.0 19.7 jit_solution(7374312510331240452)
XLA Ops:
  0.0 18.8 %shard_map.127 = (f32[1024,256]{1,0:T(8,128)S(1)}, f32[8,128]{1,0:T(8,128)S(1)}) custom-call(bf16[1024,256]{1,0:T(8,128)(2,1)} %x_hbm.1, bf16[1024,4096]{1,0:T(8,128)(2,1)} %bc_hbm.1, bf16[1024,256]{1,0:T(8,128)(2,1)} %z_hbm.1, bf16[4,1024]{1,0:T(4,128)(2,1)} %dt_hbm.1, f32[4,256]{1,0:T(4,128)} %xw_hbm.1, f32[1,256]{1,0:T(1,128)} %bitcast.4, ...), custom_call_target="tpu_custom_call" | custom-call | tf_op jit(solution)/shard_map/pallas_call | solution.py:488
  18.8 0.9 %shard_map.128 = bf16[1024,256]{1,0:T(8,128)(2,1)} custom-call(f32[1024,256]{1,0:T(8,128)S(1)} %get-tuple-element.7.gated_ref, f32[8,128]{1,0:T(8,128)S(1)} %get-tuple-element.8.scale_ref), custom_call_target="tpu_custom_call" | custom-call | tf_op jit(solution)/shard_map/pallas_call | solution.py:542

commit v7 on v4

--- a/solution.py
+++ b/solution.py
@@ -379,8 +379,8 @@
                 mix = jnp.exp2(gap) * inner[lo:hi, :hi] * step[h : h + 1, at : at + hi]
                 y = y + dot(mix.astype(BF16), x_heads[h][:hi], ((1,), (0,)))
             y_buf[at + lo : at + hi, :] = y
-        if rounds > 1 and c >= blocks - 2:
-            pass_on(0, halves[c - (blocks - 2)])
+        if rounds > 1 and blocks - 3 <= c < blocks - 1:
+            pass_on(0, halves[c - (blocks - 3)])
 
     for turn in range(1, rounds - 1):
         pass_on(turn, range(CHUNKS))

time: 18.7 us -> 19 us (1.016)
  Pallas kernels: 18.6 us -> 18.9 us
    pallas_call x1, Pallas kernels: 17.6 us -> 18 us  [shards(): pl.pallas_call(functools.partial(layer_kernel, n_ctx, n_head), out_shape=...]
where the time goes in v7:
time: 19 us; the launch traced here: 18.9 us
  Pallas kernels  18.9 us (99%)
    pallas_call x1, Pallas kernels, shards(): pl.pallas_call(functools.partial(layer_kernel, n_ctx, n_head), out_shape=...  18 us
    pallas_call x1, Pallas kernels, shards(): pl.pallas_call(scale_kernel, out_shape=jax.ShapeDtypeStruct((rows, width)...  0.92 us

profile of v7, /device:TPU:25, one launch (start us, length us, event | category | flops | bytes accessed | tf_op | source)
XLA Modules:
  0.0 18.9 jit_solution(2819484778105079809)
XLA Ops:
  0.0 18.0 %shard_map.127 = (f32[1024,256]{1,0:T(8,128)S(1)}, f32[8,128]{1,0:T(8,128)S(1)}) custom-call(bf16[1024,256]{1,0:T(8,128)(2,1)} %x_hbm.1, bf16[1024,4096]{1,0:T(8,128)(2,1)} %bc_hbm.1, bf16[1024,256]{1,0:T(8,128)(2,1)} %z_hbm.1, bf16[4,1024]{1,0:T(4,128)(2,1)} %dt_hbm.1, f32[4,256]{1,0:T(4,128)} %xw_hbm.1, f32[1,256]{1,0:T(1,128)} %bitcast.4, ...), custom_call_target="tpu_custom_call" | custom-call | tf_op jit(solution)/shard_map/pallas_call | solution.py:494
  18.0 0.9 %shard_map.128 = bf16[1024,256]{1,0:T(8,128)(2,1)} custom-call(f32[1024,256]{1,0:T(8,128)S(1)} %get-tuple-element.7.gated_ref, f32[8,128]{1,0:T(8,128)S(1)} %get-tuple-element.8.scale_ref), custom_call_target="tpu_custom_call" | custom-call | tf_op jit(solution)/shard_map/pallas_call | solution.py:548
